TPU v7x, 256 devices: a whole 4x4x8 slice. The times are simulated.
256 devices in a mesh: dp: 16 (over y, x_lo, core), tensor: 16 (over x_hi, z).
Axes of the slice: x: 4 (x_hi: 2, x_lo: 2; x = x_hi * 2 + x_lo), y: 4, z: 8, core: 2. Of those that a mesh axis runs over, the one named last changes fastest.
Arguments:
- layer_input: bfloat16 [32, 256, 4608], P('dp', 'tensor'), may hold values from -6 to 6
- out_grad: bfloat16 [32, 256, 4608], P('dp', 'tensor'), may hold values from -24 to 24
- loss_weight: float32 [32], P('dp'), may hold values from 0.1 to 1
- queries: bfloat16 [32, 256, 4096], P('dp', None, 'tensor'), may hold values from -6 to 6
- keys: bfloat16 [32, 256, 2048], P('dp', None, 'tensor'), may hold values from -6 to 6
- value_weight: bfloat16 [4608, 2048], P(None, 'tensor'), may hold values from -0.09375 to 0.09375
- output_weight: bfloat16 [4096, 4608], P('tensor'), may hold values from -0.09375 to 0.09375
- lengths: int32 [32], P('dp'), may hold values from 192 to 256, as said below
Outputs:
- grad_output: float32 [4096, 4608], P('tensor', 'dp')
- grad_value: float32 [4608, 2048], P('dp', 'tensor')
- grad_input: bfloat16 [32, 256, 4608], P('dp', 'tensor')
Inputs may be any that keep to these rules, and one draw needn't show every extreme that they name: lengths[b] real tokens stand at the front of example b; some example is full.
All inputs are finite; a program needn't handle non-finite values.
Results may differ from a plain program's by a relative error of at most 0.007.
Values may be sent and summed in bfloat16 or wider, within the bound.
A program may use at most 128 MiB of HBM per device.

v0:
```python
import jax
import jax.numpy as jnp
from jax import lax
from jax.sharding import PartitionSpec as P

D = 4608
HQ = 32
KVH = 16
HD = 128
QPRE = 144
SOFTCAP = 50


def per_device(
    layer_input, out_grad, loss_weight, queries, keys, value_weight, output_weight, lengths
):
    group = HQ // KVH
    bound = jnp.sqrt(jnp.float32(D * (HQ + KVH) * HD))
    whole_x, whole_dy = (
        lax.all_gather(layer_input, "tensor", axis=1, tiled=True),
        lax.all_gather(out_grad, "tensor", axis=1, tiled=True),
    )
    count_ex = whole_x.shape[0]
    seq_len = whole_x.shape[1]
    kv_local = keys.shape[2] // HD
    position = jnp.arange(seq_len, dtype=jnp.int32)
    live = position[None, :] < lengths[:, None]
    causal = position[None, :] <= position[:, None]
    allowed = causal[None, None, None] & live[:, None, None, None, :]
    values = jnp.einsum(
        "esd,dk->esk", whole_x, value_weight, preferred_element_type=jnp.float32
    ).astype(jnp.bfloat16)
    q_heads = queries.reshape(count_ex, seq_len, kv_local, group, HD)
    k_heads = keys.reshape(count_ex, seq_len, kv_local, HD)
    v_heads = values.reshape(count_ex, seq_len, kv_local, HD)
    raw = jnp.einsum(
        "eqkgd,eskd->ekgqs", q_heads, k_heads, preferred_element_type=jnp.float32
    ) * QPRE ** (-0.5)
    capped = SOFTCAP * jnp.tanh(raw / SOFTCAP)
    expo = jnp.where(allowed, jnp.exp(capped), 0.0)
    probs = (expo / jnp.sum(expo, axis=-1, keepdims=True)).astype(jnp.bfloat16)
    context = jnp.einsum("ekgqs,eskd->eqkgd", probs, v_heads, preferred_element_type=jnp.float32)
    context = context.astype(jnp.bfloat16).reshape(count_ex, seq_len, kv_local * group * HD)
    live_f = live.astype(jnp.float32)[:, :, None]
    grad_at_out = (whole_dy.astype(jnp.float32) * loss_weight[:, None, None] * live_f).astype(
        jnp.bfloat16
    )
    per_out = jnp.einsum("esa,esd->ead", context, grad_at_out, preferred_element_type=jnp.float32)
    part_out = jnp.sum(per_out * per_out, axis=(1, 2))
    grad_context = jnp.einsum(
        "esd,ad->esa", grad_at_out, output_weight, preferred_element_type=jnp.float32
    ).astype(jnp.bfloat16)
    grad_ctx_heads = grad_context.reshape(count_ex, seq_len, kv_local, group, HD)
    grad_values = jnp.einsum(
        "ekgqs,eqkgd->eskd", probs, grad_ctx_heads, preferred_element_type=jnp.float32
    )
    grad_values = grad_values.astype(jnp.bfloat16).reshape(count_ex, seq_len, kv_local * HD)
    per_value = jnp.einsum("esd,esk->edk", whole_x, grad_values, preferred_element_type=jnp.float32)
    part_value = jnp.sum(per_value * per_value, axis=(1, 2))
    sq_norm = lax.psum(part_out + part_value, "tensor")
    factor = bound / jnp.maximum(jnp.sqrt(sq_norm), bound)
    partial_in = jnp.einsum(
        "esk,dk->esd", grad_values, value_weight, preferred_element_type=jnp.float32
    )
    grad_input = lax.psum_scatter(partial_in, "tensor", scatter_dimension=1, tiled=True).astype(
        jnp.bfloat16
    )
    local_out = jnp.sum(factor[:, None, None] * per_out, axis=0)
    local_value = jnp.sum(factor[:, None, None] * per_value, axis=0)
    grad_output, grad_value = (
        lax.psum_scatter(local_out, "dp", scatter_dimension=1, tiled=True),
        lax.psum_scatter(local_value, "dp", scatter_dimension=0, tiled=True),
    )
    return (grad_output, grad_value, grad_input)


def solution(mesh):
    in_specs = (
        P("dp", "tensor", None),
        P("dp", "tensor", None),
        P("dp"),
        P("dp", None, "tensor"),
        P("dp", None, "tensor"),
        P(None, "tensor"),
        P("tensor", None),
        P("dp"),
    )
    out_specs = (P("tensor", "dp"), P("dp", "tensor"), P("dp", "tensor", None))
    return jax.shard_map(
        per_device, mesh=mesh, in_specs=in_specs, out_specs=out_specs, check_vma=False
    )
```

profile of v0, /device:TPU:1, one launch (start us, length us, event | category | flops | bytes accessed | tf_op | source)
XLA Modules:
  0.0 603.3 jit_solution(17396956316586802435)
XLA Ops:
  7.2 0.7 all-gather.5.cloned.1.call-update
  8.0 0.7 all-gather.3.cloned.1.call-update
  8.7 0.7 fusion.30
  9.5 0.1 broadcast_and_fusion
  9.6 2.5 fusion.31
  12.1 103.1 %all-gather.5.cloned.1.call-done = bf16[2,256,4608]{2,1,0:T(8,128)(2,1)} async-done(((bf16[2,16,4608]{2,1,0:T(8,128)(2,1)}), bf16[2,256,4608]{2,1,0:T(8,128)(2,1)}) %all-gather.5.cloned.1.call-update) | async-done | bytes 4718608 | tf_op jit(solution)/shard_map/all_gather | solution.py:21
  115.2 3.9 fusion.8
  119.1 0.3 fusion.19
  119.5 0.6 copy-done.2
  120.1 0.3 copy-done.1
  120.4 5.1 fusion.11
  125.5 92.8 %all-gather.3.cloned.1.call-done = bf16[2,256,4608]{2,1,0:T(8,128)(2,1)} async-done(((bf16[2,16,4608]{2,1,0:T(8,128)(2,1)}), bf16[2,256,4608]{2,1,0:T(8,128)(2,1)}) %all-gather.3.cloned.1.call-update) | async-done | bytes 4718608 | tf_op jit(solution)/shard_map/all_gather | solution.py:20
  218.3 5.7 multiply_reduce_fusion.3
  224.0 5.0 convolution_convert_fusion
  229.1 8.8 %multiply_reduce_fusion.1 = (f32[2]{0:T(128)S(1)}, f32[2,256,4608]{2,1,0:T(8,128)}) fusion(bf16[2,256,256]{1,2,0:T(8,128)(2,1)} %bitcast.80, bf16[2,256,4608]{2,1,0:T(8,128)(2,1)} %all-gather.5.cloned.1.call-done, f32[2,256]{1,0:T(2,128)S(1)} %get-tuple-element.9, f32[2]{0:T(128)S(1)} %copy-done.3), kind=kOutput, calls=%fused_computation.1 | convolution fusion | flops 1222115328 | bytes 14419984 | tf_op jit(solution)/shard_map/esa,esd->ead/dot_general | solution.py:48
  237.8 31.8 %psum.7 = f32[2]{0:T(128)S(1)} all-reduce(f32[2]{0:T(128)S(1)} %add.11), channel_id=1, replica_groups=mesh['dp'=16,'tensor'=16] {'tensor'}, use_global_device_ids=true, to_apply=%region_3.4 | all-reduce | flops 2 | bytes 16 | tf_op jit(solution)/shard_map/psum | solution.py:60
  269.7 4.6 multiply_reduce_fusion.2
  274.3 3.2 copy.38
  277.6 7.8 %multiply_reduce_fusion = f32[256,4608]{1,0:T(8,128)} fusion(f32[2,256,4608]{2,1,0:T(8,128)} %get-tuple-element.14, f32[2]{0:T(128)S(1)} %maximum_divide_fusion), kind=kLoop, calls=%fused_computation | loop fusion | flops 3538944 | bytes 14155784 | tf_op jit(solution)/shard_map/reduce_sum | solution.py:68
  285.4 6.1 %copy.36 = f32[256,4608]{0,1:T(8,128)} copy(f32[256,4608]{1,0:T(8,128)} %multiply_reduce_fusion) | data formatting | bytes 9437184
  291.5 159.5 %reduce-scatter.8.cloned.1.call-done = f32[2,16,4608]{2,1,0:T(8,128)} async-done(((f32[2,256,4608]{2,1,0:T(8,128)}), f32[2,16,4608]{2,1,0:T(8,128)}) %reduce-scatter.8.cloned.1.call-update) | async-done | bytes 589840 | tf_op jit(solution)/shard_map/reduce_scatter | solution.py:65
  451.0 1.8 convert_element_type.55
  452.8 68.1 %reduce-scatter.12.cloned.1.call-done = f32[288,128]{1,0:T(8,128)} async-done(((f32[4608,128]{1,0:T(8,128)}), f32[288,128]{1,0:T(8,128)}) %reduce-scatter.12.cloned.1.call-update) | async-done | bytes 147472
  520.9 75.9 %reduce-scatter.10.cloned.1.call-done = f32[288,256]{1,0:T(8,128)} async-done(((f32[4608,256]{1,0:T(8,128)}), f32[288,256]{1,0:T(8,128)}) %reduce-scatter.10.cloned.1.call-update) | async-done | bytes 294928
  (19 shorter events, 0.3 us)
Async XLA Ops:
  7.2 108.0 %copy-start = (bf16[256,4608]{1,0:T(8,128)(2,1)S(1)}, bf16[256,4608]{1,0:T(8,128)(2,1)}, u32[]{:S(2)}) copy-start(bf16[256,4608]{1,0:T(8,128)(2,1)} %param.14) | copy-start | bytes 7077892
  7.2 108.0 %all-gather.5.cloned.1.call-start = ((), (), s32[]{:S(2)}) async-start(), calls=%async_computation.4 | async-start | bytes 5013504 | tf_op jit(solution)/shard_map/all_gather | solution.py:21
  7.9 210.4 %all-gather.3.cloned.1.call-start = ((), (), s32[]{:S(2)}) async-start(), calls=%async_computation.3 | async-start | bytes 5013504 | tf_op jit(solution)/shard_map/all_gather | solution.py:20
  8.7 442.3 %reduce-scatter.8.cloned.1.call-start = ((), (), s32[]{:S(2)}) async-start(), calls=%async_computation.5 | async-start | bytes 10027008 | tf_op jit(solution)/shard_map/reduce_scatter | solution.py:65
  115.2 3.9 copy-start.4
  119.1 1.3 copy-start.1
  119.5 0.7 copy-start.2
  125.5 395.4 %reduce-scatter.12.cloned.1.call-start = ((), (), s32[]{:S(2)}) async-start(), calls=%async_computation.7 | async-start | bytes 2506752
  224.0 5.0 copy-start.3
  277.5 319.3 %reduce-scatter.10.cloned.1.call-start = ((), (), s32[]{:S(2)}) async-start(), calls=%async_computation.6 | async-start | bytes 5013504
Sparse Core Ops, SparseCore 0:
  10.6 104.5 all-gather.4
  117.8 100.4 all-gather.2
  222.5 228.3 reduce-scatter.7
  454.1 66.7 reduce-scatter.11
  524.0 72.7 reduce-scatter.9
where the time goes:
time: 605 us; the launch traced here: 603 us
  waiting for transfers between devices  501 us (83%)
  blocking collectives  31.8 us (5%)
  matrix products  31.3 us (5%)
  other arithmetic  15.1 us (2%)
  between operations  13.8 us (2%)
  local copies, waits for them, and re-layouts  10.2 us (2%)
    reduce_scatter x1, waiting for transfers between devices, per_device(): lax.psum_scatter(partial_in, 'tensor', scatter_dimension=1, tiled=True)  159 us
    unnamed x7, waiting for transfers between devices  145 us
    all_gather x1, waiting for transfers between devices, per_device(): lax.all_gather(out_grad, 'tensor', axis=1, tiled=True)  103 us
    all_gather x1, waiting for transfers between devices, per_device(): lax.all_gather(layer_input, 'tensor', axis=1, tiled=True)  92.8 us
    psum x1, blocking collectives, per_device(): sq_norm = lax.psum(part_out + part_value, 'tensor')  31.8 us
  transfers between devices with their start and end apart: 5, of which 5 were waited for; matrix products, arithmetic and copies ran while one was open for 9% of the time, Pallas kernels for 0%

commit v1 on v0

v1 whole, which is shorter than its diff:
```python
import jax
import jax.numpy as jnp
from jax import lax
from jax.experimental import pallas as pl
from jax.experimental.pallas import tpu as pltpu
from jax.sharding import PartitionSpec as P

D = 4608
HQ = 32
KVH = 16
HD = 128
QPRE = 144
SOFTCAP = 50
SEQ = 256
NZ = 8
TOK = 16
HALF = D // 2
MESH = pl.DeviceIdType.MESH
F32 = jnp.float32
BF16 = jnp.bfloat16


def mo(value, multiple):
    return pl.multiple_of(value, multiple)


def dot(a, b):
    return jnp.dot(a, b, preferred_element_type=F32)


def kernel(
    lw_ref, len_ref, x_ref, g_ref, q_ref, k_ref, wv_ref, wo_ref,
    outt_ref, val_ref, gi_ref,
    xall, gall, xt, gt, gsend, qall, kall, wv, wvt, wo, probs, vall, call, dct, dvt, dv,
    gram, nbuf, dxf, zs, zr, gis, gir, csend, crecv, ssum,
    a1r, a2s, a2r, ua, a4r, a5s, a5r, b1r, b2s, b2r, ub, b4r, b5s, b5r,
    lsem, xsem, agsem, wsem, nsem, zsem, csem, rsem,
):
    dp, tn = lax.axis_index("dp"), lax.axis_index("tensor")
    h, z = lax.div(tn, NZ), lax.rem(tn, NZ)
    y, l, c = lax.div(dp, 4), lax.rem(lax.div(dp, 2), 2), lax.rem(dp, 2)
    x = 2 * h + l
    oh = 1 - h

    def zdev(step):
        return (dp, h * NZ + lax.rem(z + step + NZ, NZ))

    def ydev(step):
        return (lax.rem(y + step + 4, 4) * 4 + l * 2 + c, tn)

    def xpos(step):
        return lax.rem(x + step + 4, 4)

    def xdev(step):
        there = xpos(step)
        return (y * 4 + lax.rem(there, 2) * 2 + c, lax.div(there, 2) * NZ + z)

    partner = (dp, oh * NZ + z)
    cross = (y * 4 + (1 - l) * 2 + c, oh * NZ + z)
    core = (dp + 1 - 2 * c, tn)

    def rows(hs, zz):
        return pl.ds(mo(hs * (NZ * TOK) + zz * TOK, TOK), TOK)

    def remote(src, dst, sem, index, device):
        return pltpu.make_async_remote_copy(
            src_ref=src, dst_ref=dst, send_sem=sem.at[0, index], recv_sem=sem.at[1, index],
            device_id=device, device_id_type=MESH,
        )

    sent = []

    def send(src, dst, sem, index, device):
        copy = remote(src, dst, sem, index, device)
        copy.start()
        sent.append(copy)

    def arrived(dst, sem, index, device):
        remote(dst, dst, sem, index, device).wait_recv()

    my_rows, other_rows = rows(h, z), rows(oh, z)
    local = [
        pltpu.make_async_copy(x_ref.at[h], xall.at[my_rows], lsem.at[0]),
        pltpu.make_async_copy(q_ref.at[h], qall.at[:, pl.ds(mo(h * 256, 256), 256)], lsem.at[1]),
        pltpu.make_async_copy(k_ref.at[h], kall.at[:, pl.ds(mo(h * 128, 128), 128)], lsem.at[2]),
        pltpu.make_async_copy(wv_ref, wv.at[:, pl.ds(mo(h * 128, 128), 128)], lsem.at[3]),
        pltpu.make_async_copy(wo_ref, wo.at[pl.ds(mo(h * 256, 256), 256)], lsem.at[4]),
    ]
    for copy in local:
        copy.start()

    barrier = pltpu.get_barrier_semaphore()
    peers = [zdev(k) for k in range(1, NZ)] + [ydev(1), ydev(-1), xdev(1), xdev(-1), partner, core]
    for peer in peers:
        pl.semaphore_signal(barrier, inc=1, device_id=peer, device_id_type=MESH)

    position = tn * TOK + lax.broadcasted_iota(jnp.int32, (TOK, 1), 0)

    def weighted(e):
        live = (position < len_ref[e]).astype(F32)
        return (g_ref[e].astype(F32) * lw_ref[e] * live).astype(BF16)

    gall[my_rows, :] = weighted(h)
    gsend[...] = weighted(oh)

    pl.semaphore_wait(barrier, len(peers))

    arrs = (xall, gall)

    def ag_ref(arr, part, way, k, received):
        hs = h if part == 0 else oh
        back = k if received else k - 1
        origin = lax.rem(z + (NZ - back if way == 0 else back), NZ)
        columns = slice(None)
        if k == 4:
            columns = pl.ds(0, HALF) if way == 0 else pl.ds(HALF, HALF)
        return arrs[arr].at[rows(hs, origin), columns]

    def ag_index(arr, part, way, k):
        return ((arr * 2 + part) * 2 + way) * 4 + k - 1

    def ag_send(arr, part, k):
        for way in range(2):
            ref = ag_ref(arr, part, way, k, False)
            send(ref, ref, agsem, ag_index(arr, part, way, k), zdev(1 - 2 * way))

    def ag_wait(arr, part, k):
        for way in range(2):
            arrived(ag_ref(arr, part, way, k, True), agsem, ag_index(arr, part, way, k), zdev(1 - 2 * way))

    def ag_next(arr, part, k):
        ag_wait(arr, part, k)
        ag_send(arr, part, k + 1)

    def ex_refs(k, mine):
        hs = h if mine else oh
        qcol, kcol = pl.ds(mo(hs * 256, 256), 256), pl.ds(mo(hs * 128, 128), 128)
        return (
            xall.at[rows(hs, z)], gall.at[rows(hs, z)], qall.at[:, qcol], kall.at[:, kcol],
            gir,
        )[k]

    def ex_send(k, src):
        send(src, ex_refs(k, True), xsem, k, partner)

    def ex_wait(k):
        arrived(ex_refs(k, False), xsem, k, partner)

    def w_ref(arr, hs, yy, cc, part=None):
        piece = yy * 2 + cc
        size = (D // 8, 32)[arr]
        start = piece * size
        if part is not None:
            size = size // 2
            start = start + part * size
        ds = pl.ds(mo(start, 16), size)
        if arr == 0:
            return wv.at[ds, pl.ds(mo(hs * 128, 128), 128)]
        return wo.at[pl.ds(mo(hs * 256 + start, 16), size)]

    def w_first(arr):
        piece = y * 2 + c
        size = (D // 8, 32)[arr]
        src = (wv_ref, wo_ref)[arr].at[pl.ds(mo(piece * size, 16), size)]
        send(src, w_ref(arr, h, y, c), wsem, arr * 9, cross)

    def w_core(arr, step):
        yy = lax.rem(y + step, 4)
        ref = w_ref(arr, oh, yy, c)
        send(ref, ref, wsem, arr * 9 + 5 + step, core)

    def w_second(arr):
        ref = w_ref(arr, oh, y, c)
        arrived(ref, wsem, arr * 9, cross)
        send(ref, ref, wsem, arr * 9 + 1, ydev(1))
        send(ref, ref, wsem, arr * 9 + 2, ydev(-1))
        w_core(arr, 0)

    def w_third(arr):
        low, high = lax.rem(y + 3, 4), lax.rem(y + 1, 4)
        arrived(w_ref(arr, oh, low, c), wsem, arr * 9 + 1, ydev(1))
        ref = w_ref(arr, oh, low, c, 0)
        send(ref, ref, wsem, arr * 9 + 3, ydev(1))
        arrived(w_ref(arr, oh, high, c), wsem, arr * 9 + 2, ydev(-1))
        ref = w_ref(arr, oh, high, c, 1)
        send(ref, ref, wsem, arr * 9 + 4, ydev(-1))
        w_core(arr, 3)
        w_core(arr, 1)

    def w_fourth(arr):
        far = lax.rem(y + 2, 4)
        arrived(w_ref(arr, oh, far, c, 0), wsem, arr * 9 + 3, ydev(1))
        arrived(w_ref(arr, oh, far, c, 1), wsem, arr * 9 + 4, ydev(-1))
        w_core(arr, 2)

    def w_last(arr):
        for step in range(4):
            arrived(w_ref(arr, oh, lax.rem(y + step, 4), 1 - c), wsem, arr * 9 + 5 + step, core)

    def softmax(hs):
        length = len_ref[h]
        qpos = lax.broadcasted_iota(jnp.int32, (SEQ, SEQ), 0)
        kpos = lax.broadcasted_iota(jnp.int32, (SEQ, SEQ), 1)
        allowed = (kpos <= qpos) & (kpos < length)
        keys = kall[:, pl.ds(mo(hs * 128, 128), 128)]
        for g in range(2):
            query = qall[:, pl.ds(mo(hs * 256 + g * 128, 128), 128)]
            raw = lax.dot_general(query, keys, (((1,), (1,)), ((), ())), preferred_element_type=F32)
            capped = SOFTCAP * jnp.tanh(raw * (QPRE ** -0.5 / SOFTCAP))
            expo = jnp.where(allowed, jnp.exp(capped), 0.0)
            total = jnp.sum(expo, axis=1, keepdims=True)
            probs[hs * 2 + g] = (expo / total).astype(BF16)

    def transpose_half(src, dst, part):
        hs = h if part == 0 else oh
        ds = pl.ds(mo(hs * 128, 128), 128)

        def step(i, carry):
            cols = pl.ds(mo(i * 128, 128), 128)
            dst[cols, ds] = src[ds, cols].T
            return carry

        lax.fori_loop(0, D // 128, step, 0)

    def values(part):
        hs = h if part == 0 else oh
        ds = pl.ds(mo(hs * 128, 128), 128)
        vall[ds, :] = dot(xall[ds, :], wv[...]).astype(BF16)

    def contexts():
        for head in range(4):
            kv = head // 2
            call[:, head * 128:(head + 1) * 128] = dot(
                probs[head], vall[:, kv * 128:(kv + 1) * 128]
            ).astype(BF16)

    def wv_turn():
        def step(i, carry):
            ds = pl.ds(mo(i * 128, 128), 128)
            wvt[:, ds] = wv[ds, :].T
            return carry

        lax.fori_loop(0, D // 128, step, 0)

    def grad_contexts(part):
        hs = h if part == 0 else oh
        ds = pl.ds(mo(hs * 128, 128), 128)
        for half in range(2):
            dct[half * 256:(half + 1) * 256, ds] = dot(
                wo[half * 256:(half + 1) * 256, :], gt[:, ds]
            ).astype(BF16)

    def grad_values():
        for kv in range(2):
            both = dot(dct[kv * 256:kv * 256 + 128, :], probs[2 * kv])
            both += dot(dct[kv * 256 + 128:kv * 256 + 256, :], probs[2 * kv + 1])
            dvt[kv * 128:(kv + 1) * 128, :] = both.astype(BF16)
        dv[...] = dvt[...].T

    def x_gram():
        gram[...] = dot(xall[...], xt[...])

    def norm_send():
        cgram = lax.dot_general(call[...], call[...], (((1,), (1,)), ((), ())), preferred_element_type=F32)
        total = cgram * dot(gall[...], gt[...]) + gram[...] * dot(dv[...], dvt[...])
        total = jnp.sum(jnp.sum(total, axis=0, keepdims=True), axis=1, keepdims=True)
        nbuf[z] = jnp.broadcast_to(total, (8, 128))
        for k in range(1, NZ):
            send(nbuf.at[z], nbuf.at[z], nsem, k - 1, zdev(k))

    def norm_wait():
        for k in range(1, NZ):
            arrived(nbuf.at[lax.rem(z + NZ - k, NZ)], nsem, k - 1, zdev(k))
        sq = jnp.sum(nbuf[...], axis=0)[0:1, 0:1]
        bound = jnp.sqrt(F32(D * (HQ + KVH) * HD))
        return bound / jnp.maximum(jnp.sqrt(sq), bound)

    def dx_partial(part):
        hs = h if part == 0 else oh
        ds = pl.ds(mo(hs * 128, 128), 128)

        def step(i, carry):
            cols = pl.ds(mo(i * 512, 512), 512)
            dxf[ds, cols] = dot(dv[ds, :], wvt[:, cols])
            return carry

        lax.fori_loop(0, D // 512, step, 0)

    def z_cols(way):
        return pl.ds(0, HALF) if way == 0 else pl.ds(HALF, HALF)

    def z_index(part, way, k):
        return (part * 2 + way) * 4 + k - 1

    def z_start(part, way, k):
        index = z_index(part, way, k)
        src, dst = zs.at[index], zr.at[index]
        if k == 1:
            src, dst = src.at[:, z_cols(way)], dst.at[:, z_cols(way)]
        send(src, dst, zsem, index, zdev(1 - 2 * way))

    def z_arrived(part, way, k):
        index = z_index(part, way, k)
        dst = zr.at[index]
        if k == 1:
            dst = dst.at[:, z_cols(way)]
        arrived(dst, zsem, index, zdev(1 - 2 * way))

    def z_step(part, k):
        hs = h if part == 0 else oh
        for way in range(2):
            hops = 5 - k
            target = rows(hs, lax.rem(z + (hops if way == 0 else NZ - hops), NZ))
            index = z_index(part, way, k)
            if k == 1:
                zs[index, :, z_cols(way)] = dxf[target, z_cols(way)].astype(BF16)
            else:
                z_arrived(part, way, k - 1)
                if k == 2:
                    mine, rest = z_cols(way), z_cols(1 - way)
                    zs[index, :, mine] = (dxf[target, mine] + zr[index - 1, :, mine].astype(F32)).astype(BF16)
                    zs[index, :, rest] = dxf[target, rest].astype(BF16)
                else:
                    zs[index] = (dxf[target, :] + zr[index - 1].astype(F32)).astype(BF16)
            z_start(part, way, k)

    def z_final(part):
        hs = h if part == 0 else oh
        for way in range(2):
            z_arrived(part, way, 4)
        total = dxf[rows(hs, z), :]
        for way in range(2):
            total += zr[z_index(part, way, 4)].astype(F32)
        return total.astype(BF16)

    def grad_block(index, factor):
        ds = pl.ds(mo(index * 288, 16), 288)
        out = dot(gt[ds, :], call[...]) * factor
        value = dot(xt[ds, :], dv[...]) * factor
        return ((0, out[:, :256]), (256, value[:, :128]), (384, out[:, 256:]), (640, value[:, 128:]))

    def core_copy(n):
        return remote(csend.at[n], crecv.at[n], csem, n, core)

    def core_send(n, factor):
        for start, piece in grad_block(2 * n + 1 - c, factor):
            csend[n, :, start:start + piece.shape[1]] = piece.astype(BF16)
        core_copy(n).start()

    def core_sum(n, factor):
        core_copy(n).wait()
        for start, piece in grad_block(2 * n + c, factor):
            cols = slice(start, start + piece.shape[1])
            ssum[n, :, cols] = (piece + crecv[n, :, cols].astype(F32)).astype(BF16)

    def add(*pieces):
        total = pieces[0].astype(F32)
        for piece in pieces[1:]:
            total += piece.astype(F32)
        return total

    LOW, HIGH = pl.ds(0, 144), pl.ds(144, 144)

    def yp(step):
        return lax.rem(y + step + 4, 4)

    def hcols(hh):
        return pl.ds(mo(hh * 384, 128), 384)

    def xhl(step):
        there = xpos(step)
        return lax.div(there, 2), lax.rem(there, 2)

    def a_one():
        far = yp(2)
        send(ssum.at[2 * far, LOW], a1r.at[0], rsem, 0, ydev(1))
        send(ssum.at[2 * far + 1, LOW], a1r.at[1], rsem, 1, ydev(-1))
        send(ssum.at[2 * yp(1) + 1, LOW], a2r.at[0, 1], rsem, 2, ydev(1))
        send(ssum.at[2 * yp(-1), LOW], a2r.at[1, 0], rsem, 3, ydev(-1))

    def a_two():
        for way in range(2):
            step = 1 - 2 * way
            arrived(a1r.at[way], rsem, way, ydev(step))
            a2s[way] = add(ssum[2 * yp(step) + way, LOW, :], a1r[way]).astype(BF16)
            send(a2s.at[way], a2r.at[way, way], rsem, 4 + way, ydev(step))

    def a_three():
        arrived(a2r.at[0, 1], rsem, 2, ydev(1))
        arrived(a2r.at[1, 0], rsem, 3, ydev(-1))
        for way in range(2):
            arrived(a2r.at[way, way], rsem, 4 + way, ydev(1 - 2 * way))
        for ll in range(2):
            ua[ll] = add(ssum[2 * y + ll, LOW, :], a2r[0, ll], a2r[1, ll]).astype(BF16)
        ph, pll = xhl(2)
        send(ua.at[pll, pl.ds(0, 80), hcols(ph)], a4r.at[pl.ds(0, 80)], rsem, 6, xdev(1))
        send(ua.at[pll, pl.ds(80, 64), hcols(ph)], a4r.at[pl.ds(80, 64)], rsem, 7, xdev(-1))

    def a_four():
        for way, (start, size) in enumerate(((0, 80), (80, 64))):
            step = 1 - 2 * way
            ds, other = pl.ds(start, size), (pl.ds(80, 64), pl.ds(0, 80))[way]
            ph, pll = xhl(step)
            arrived(a4r.at[ds], rsem, 6 + way, xdev(step))
            a5s[way, ds, :] = add(ua[pll, ds, hcols(ph)], a4r[ds, :]).astype(BF16)
            a5s[way, other, :] = ua[pll, other, hcols(ph)]
            send(a5s.at[way], a5r.at[way], rsem, 8 + way, xdev(step))

    def a_five():
        for way in range(2):
            arrived(a5r.at[way], rsem, 8 + way, xdev(1 - 2 * way))
        total = add(ua[l, :, hcols(h)], a5r[0], a5r[1])
        outt_ref[0:144, :] = total[:, :256]
        val_ref[0:144, :] = total[:, 256:]

    def s_high(yy, ll, hh):
        return ssum.at[2 * yy + ll, HIGH, hcols(hh)]

    def b_one():
        ph, pll = xhl(2)
        for yy in range(4):
            send(s_high(yy, pll, ph), b1r.at[yy], rsem, 10 + yy, xdev(1 if yy < 2 else -1))
        for yy in range(4):
            way = 1 if yy < 2 else 0
            ph, pll = xhl(1 - 2 * way)
            send(s_high(yy, pll, ph), b2r.at[way, yy], rsem, 14 + yy, xdev(1 - 2 * way))

    def b_two():
        for yy in range(4):
            way = 0 if yy < 2 else 1
            step = 1 - 2 * way
            ph, pll = xhl(step)
            arrived(b1r.at[yy], rsem, 10 + yy, xdev(step))
            b2s[yy] = add(ssum[2 * yy + pll, HIGH, hcols(ph)], b1r[yy]).astype(BF16)
            send(b2s.at[yy], b2r.at[way, yy], rsem, 18 + yy, xdev(step))

    def b_three():
        for yy in range(4):
            way = 1 if yy < 2 else 0
            arrived(b2r.at[way, yy], rsem, 14 + yy, xdev(1 - 2 * way))
            arrived(b2r.at[1 - way, yy], rsem, 18 + yy, xdev(2 * way - 1))
            ub[yy] = add(ssum[2 * yy + l, HIGH, hcols(h)], b2r[0, yy], b2r[1, yy]).astype(BF16)
        far = yp(2)
        send(ub.at[far, pl.ds(0, 80)], b4r.at[pl.ds(0, 80)], rsem, 22, ydev(1))
        send(ub.at[far, pl.ds(80, 64)], b4r.at[pl.ds(80, 64)], rsem, 23, ydev(-1))

    def b_four():
        for way, (start, size) in enumerate(((0, 80), (80, 64))):
            step = 1 - 2 * way
            ds, other = pl.ds(start, size), (pl.ds(80, 64), pl.ds(0, 80))[way]
            arrived(b4r.at[ds], rsem, 22 + way, ydev(step))
            b5s[way, ds, :] = add(ub[yp(step), ds, :], b4r[ds, :]).astype(BF16)
            b5s[way, other, :] = ub[yp(step), other, :]
            send(b5s.at[way], b5r.at[way], rsem, 24 + way, ydev(step))

    def b_five():
        for way in range(2):
            arrived(b5r.at[way], rsem, 24 + way, ydev(1 - 2 * way))
        total = add(ub[y], b5r[0], b5r[1])
        outt_ref[144:288, :] = total[:, :256]
        val_ref[144:288, :] = total[:, 256:]

    X, G, OWN, OTHER = 0, 1, 0, 1
    ex_send(0, x_ref.at[oh])
    local[0].wait()
    ag_send(X, OWN, 1)
    ex_send(1, gsend)
    ag_send(G, OWN, 1)
    w_first(0)
    ex_send(2, q_ref.at[oh])
    ex_send(3, k_ref.at[oh])
    w_first(1)
    local[1].wait()
    local[2].wait()
    ag_next(X, OWN, 1)
    ex_wait(0)
    ag_send(X, OTHER, 1)
    softmax(h)
    ag_next(X, OWN, 2)
    w_second(0)
    ag_next(X, OTHER, 1)
    ag_next(G, OWN, 1)
    ag_next(X, OWN, 3)
    w_third(0)
    ag_next(X, OTHER, 2)
    ex_wait(1)
    ag_send(G, OTHER, 1)
    w_second(1)
    ex_wait(2)
    ex_wait(3)
    softmax(oh)
    w_fourth(0)
    ag_next(X, OTHER, 3)
    ag_next(G, OWN, 2)
    ag_wait(X, OWN, 4)
    transpose_half(xall, xt, OWN)
    w_third(1)
    ag_next(G, OTHER, 1)
    w_last(0)
    local[3].wait()
    values(OWN)
    ag_next(G, OWN, 3)
    w_fourth(1)
    ag_next(G, OTHER, 2)
    ag_wait(X, OTHER, 4)
    transpose_half(xall, xt, OTHER)
    values(OTHER)
    ag_next(G, OTHER, 3)
    contexts()
    wv_turn()
    w_last(1)
    local[4].wait()
    ag_wait(G, OWN, 4)
    transpose_half(gall, gt, OWN)
    grad_contexts(OWN)
    x_gram()
    ag_wait(G, OTHER, 4)
    transpose_half(gall, gt, OTHER)
    grad_contexts(OTHER)
    grad_values()
    dx_partial(OTHER)
    z_step(OTHER, 1)
    norm_send()
    dx_partial(OWN)
    z_step(OWN, 1)
    z_step(OTHER, 2)
    factor = norm_wait()
    z_step(OWN, 2)

    def first(n, carry):
        core_send(n, factor)
        return carry

    def second(n, carry):
        core_sum(n, factor)
        return carry

    lax.fori_loop(0, 8, first, 0)
    z_step(OTHER, 3)
    lax.fori_loop(0, 8, second, 0)
    a_one()
    b_one()
    z_step(OWN, 3)
    a_two()
    b_two()
    z_step(OTHER, 4)
    z_step(OWN, 4)
    a_three()
    b_three()
    a_four()
    b_four()
    gis[...] = z_final(OTHER)
    ex_send(4, gis)
    a_five()
    b_five()
    gi_ref[h] = z_final(OWN)
    ex_wait(4)
    gi_ref[oh] = gir[...]
    for copy in sent:
        copy.wait_send()


def per_device(layer_input, out_grad, loss_weight, queries, keys, value_weight, output_weight, lengths):
    any_spec = pl.BlockSpec(memory_space=pl.ANY)
    smem = pl.BlockSpec(memory_space=pltpu.SMEM)
    vmem = pl.BlockSpec(memory_space=pltpu.VMEM)

    def buf(*shape, dtype=BF16):
        return pltpu.VMEM(shape, dtype)

    dma = pltpu.SemaphoreType.DMA
    out_t, value, grad_input = pl.pallas_call(
        kernel,
        out_shape=(
            jax.ShapeDtypeStruct((288, 256), F32),
            jax.ShapeDtypeStruct((288, 128), F32),
            jax.ShapeDtypeStruct((2, TOK, D), BF16),
        ),
        in_specs=[smem, smem, any_spec, vmem, any_spec, any_spec, any_spec, any_spec],
        out_specs=(vmem, vmem, vmem),
        scratch_shapes=[
            buf(SEQ, D), buf(SEQ, D), buf(D, SEQ), buf(D, SEQ), buf(TOK, D),
            buf(SEQ, 512), buf(SEQ, 256), buf(D, 256), buf(256, D), buf(512, D),
            buf(4, SEQ, SEQ), buf(SEQ, 256), buf(SEQ, 512), buf(512, SEQ), buf(256, SEQ), buf(SEQ, 256),
            buf(SEQ, SEQ, dtype=F32), buf(NZ, 8, 128, dtype=F32), buf(SEQ, D, dtype=F32),
            buf(16, TOK, D), buf(16, TOK, D), buf(TOK, D), buf(TOK, D),
            buf(8, 288, 768), buf(8, 288, 768), buf(8, 288, 768),
            buf(2, 144, 768), buf(2, 144, 768), buf(2, 2, 144, 768), buf(2, 144, 768),
            buf(144, 384), buf(2, 144, 384), buf(2, 144, 384),
            buf(4, 144, 384), buf(4, 144, 384), buf(2, 4, 144, 384), buf(4, 144, 384),
            buf(144, 384), buf(2, 144, 384), buf(2, 144, 384),
            dma((5,)), dma((2, 5)), dma((2, 32)), dma((2, 18)), dma((2, 7)), dma((2, 16)), dma((2, 8)),
            dma((2, 26)),
        ],
        compiler_params=pltpu.CompilerParams(
            collective_id=0, has_side_effects=True, vmem_limit_bytes=60 * 1024 * 1024
        ),
        cost_estimate=pl.CostEstimate(flops=5_000_000_000, bytes_accessed=12_000_000, transcendentals=1_000_000),
        name="clipped_grads",
    )(loss_weight, lengths, layer_input, out_grad, queries, keys, value_weight, output_weight)
    return out_t.T, value, grad_input


def solution(mesh):
    in_specs = (
        P("dp", "tensor", None),
        P("dp", "tensor", None),
        P("dp"),
        P("dp", None, "tensor"),
        P("dp", None, "tensor"),
        P(None, "tensor"),
        P("tensor", None),
        P("dp"),
    )
    out_specs = (P("tensor", "dp"), P("dp", "tensor"), P("dp", "tensor", None))
    return jax.shard_map(
        per_device, mesh=mesh, in_specs=in_specs, out_specs=out_specs, check_vma=False
    )
```

time: 605 us -> 121 us (0.20)
  waiting for transfers between devices: 501 us -> 0 us
  Pallas kernels: 0 us -> 116 us
  blocking collectives: 31.8 us -> 0 us
  matrix products: 31.3 us -> 0 us
  other arithmetic: 15.1 us -> 0 us
  between operations: 13.8 us -> 0.64 us
    all_gather x2 -> x0, waiting for transfers between devices: 196 us -> none  [the longest x1 103 us: per_device(): lax.all_gather(out_grad, 'tensor', axis=1, tiled=True)]
    reduce_scatter x1 -> x0, waiting for transfers between devices: 159 us -> none  [per_device(): lax.psum_scatter(partial_in, 'tensor', scatter_dimension=1, tiled=True)]
    unnamed x7 -> x0, waiting for transfers between devices: 145 us -> none
    pallas_call x0 -> x1, Pallas kernels: none -> 116 us  [per_device(): pl.pallas_call(kernel, out_shape=(jax.ShapeDtypeStruct((288, 256), F32),...]
    psum x1 -> x0, blocking collectives: 31.8 us -> none  [per_device(): sq_norm = lax.psum(part_out + part_value, 'tensor')]
    dot_general x7 -> x0, matrix products: 31.3 us -> none  [the longest x1 8.79 us: per_device(): jnp.einsum('esa,esd->ead', context, grad_at_out, preferred_element_type=j...]
    reduce_sum x2 -> x0, other arithmetic: 12.4 us -> none  [the longest x1 7.79 us: per_device(): local_out = jnp.sum(factor[:, None, None] * per_out, axis=0)]
  transfers between devices with their start and end apart: 5 -> 0, of which waited for: 5 -> 0; matrix products, arithmetic and copies ran while one was open for 9% -> 0% of each run, Pallas kernels for 0% -> 0%
where the time goes in v1:
time: 121 us
  Pallas kernels  116 us (96%)
  local copies, waits for them, and re-layouts  4.97 us (4%)
    pallas_call x1, Pallas kernels, per_device(): pl.pallas_call(kernel, out_shape=(jax.ShapeDtypeStruct((288, 256), F32),...  116 us
    unnamed x3, local copies, waits for them, and re-layouts  4.97 us

profile of v1, /device:TPU:1, one launch (start us, length us, event | category | flops | bytes accessed | tf_op | source)
XLA Modules:
  0.0 121.2 jit_solution(1267576935137024213)
XLA Ops:
  0.6 115.5 %clipped_grads.1 = (f32[288,256]{1,0:T(8,128)}, f32[288,128]{1,0:T(8,128)}, bf16[2,16,4608]{2,1,0:T(8,128)(2,1)}) custom-call(f32[2]{0:T(128)} %lw_ref.1, s32[2]{0:T(128)} %len_ref.1, bf16[2,16,4608]{2,1,0:T(8,128)(2,1)} %x_ref.1, bf16[2,16,4608]{2,1,0:T(8,128)(2,1)} %g_ref.1, bf16[2,256,256]{2,1,0:T(8,128)(2,1)} %q_ref.1, bf16[2,256,128]{2,1,0:T(8,128)(2,1)} %k_ref.1, ...), custom_call_target="tpu_custom_call" | custom-call | flops 5000000000 | bytes 12000000 | tf_op jit(solution)/shard_map/clipped_grads/pallas_call | solution.py:572
  116.2 1.7 %copy.14 = f32[256,288]{0,1:T(8,128)} copy(f32[256,288]{0,1:T(8,128)} %bitcast.1) | data formatting | bytes 589824
  117.9 1.6 %copy.15 = f32[288,128]{1,0:T(8,128)} copy(f32[288,128]{1,0:T(8,128)} %get-tuple-element.13) | data formatting | bytes 294912
  119.5 1.7 %copy.16 = bf16[2,16,4608]{2,1,0:T(8,128)(2,1)} copy(bf16[2,16,4608]{2,1,0:T(8,128)(2,1)} %get-tuple-element.14) | data formatting | bytes 589824

commit v2 on v1

--- a/solution.py
+++ b/solution.py
@@ -31,11 +31,12 @@
 def kernel(
     lw_ref, len_ref, x_ref, g_ref, q_ref, k_ref, wv_ref, wo_ref,
     outt_ref, val_ref, gi_ref,
-    xall, gall, xt, gt, gsend, qall, kall, wv, wvt, wo, probs, vall, call, dct, dvt, dv,
-    gram, nbuf, dxf, zs, zr, gis, gir, csend, crecv, ssum,
-    a1r, a2s, a2r, ua, a4r, a5s, a5r, b1r, b2s, b2r, ub, b4r, b5s, b5r,
+    xall, gall, xt4, gt4, xtp, gtp, gsend, qall, kall, wv, wo, probs, vall, call, callp, dct, dvt, dv, dvp,
+    gram, xgram, nbuf, fbuf, dxf, zs, zr, gis, gir, ssum,
+    a1r, a2s, a2r, ua, a4r, b1r, b2s, b2r, ub, b4r,
     lsem, xsem, agsem, wsem, nsem, zsem, csem, rsem,
 ):
+    xt, gt = xt4.reshape(D, SEQ), gt4.reshape(D, SEQ)
     dp, tn = lax.axis_index("dp"), lax.axis_index("tensor")
     h, z = lax.div(tn, NZ), lax.rem(tn, NZ)
     y, l, c = lax.div(dp, 4), lax.rem(lax.div(dp, 2), 2), lax.rem(dp, 2)
@@ -90,7 +91,7 @@
         copy.start()
 
     barrier = pltpu.get_barrier_semaphore()
-    peers = [zdev(k) for k in range(1, NZ)] + [ydev(1), ydev(-1), xdev(1), xdev(-1), partner, core]
+    peers = [zdev(1), zdev(-1), ydev(1), ydev(-1), xdev(1), xdev(-1), xdev(2), ydev(2), core]
     for peer in peers:
         pl.semaphore_signal(barrier, inc=1, device_id=peer, device_id_type=MESH)
 
@@ -103,8 +104,8 @@
     gall[my_rows, :] = weighted(h)
     gsend[...] = weighted(oh)
 
-    pl.semaphore_wait(barrier, len(peers))
-
+
+    X, G, OWN, OTHER = 0, 1, 0, 1
     arrs = (xall, gall)
 
     def ag_ref(arr, part, way, k, received):
@@ -216,11 +217,11 @@
         ds = pl.ds(mo(hs * 128, 128), 128)
 
         def step(i, carry):
-            cols = pl.ds(mo(i * 128, 128), 128)
+            cols = pl.ds(mo(i * 512, 512), 512)
             dst[cols, ds] = src[ds, cols].T
             return carry
 
-        lax.fori_loop(0, D // 128, step, 0)
+        lax.fori_loop(0, D // 512, step, 0)
 
     def values(part):
         hs = h if part == 0 else oh
@@ -234,14 +235,6 @@
                 probs[head], vall[:, kv * 128:(kv + 1) * 128]
             ).astype(BF16)
 
-    def wv_turn():
-        def step(i, carry):
-            ds = pl.ds(mo(i * 128, 128), 128)
-            wvt[:, ds] = wv[ds, :].T
-            return carry
-
-        lax.fori_loop(0, D // 128, step, 0)
-
     def grad_contexts(part):
         hs = h if part == 0 else oh
         ds = pl.ds(mo(hs * 128, 128), 128)
@@ -257,13 +250,25 @@
             dvt[kv * 128:(kv + 1) * 128, :] = both.astype(BF16)
         dv[...] = dvt[...].T
 
+    def nt(a, b):
+        return lax.dot_general(a, b, (((1,), (1,)), ((), ())), preferred_element_type=F32)
+
+    def g_gram():
+        gram[...] = dot(gall[...], gt[...])
+
     def x_gram():
-        gram[...] = dot(xall[...], xt[...])
+        ds = pl.ds(mo(h * 128, 128), 128)
+        xgram[...] = nt(xall[ds, :], xall[ds, :]) * nt(dv[ds, :], dv[ds, :])
 
     def norm_send():
-        cgram = lax.dot_general(call[...], call[...], (((1,), (1,)), ((), ())), preferred_element_type=F32)
-        total = cgram * dot(gall[...], gt[...]) + gram[...] * dot(dv[...], dvt[...])
-        total = jnp.sum(jnp.sum(total, axis=0, keepdims=True), axis=1, keepdims=True)
+        ds = pl.ds(mo(oh * 128, 128), 128)
+        column = lax.broadcasted_iota(jnp.int32, (128, SEQ), 1)
+        twice = jnp.where(lax.div(column, 128) == h, 2.0, 1.0)
+        rest = nt(xall[ds, :], xall[...]) * nt(dv[ds, :], dv[...]) * twice
+        total = jnp.sum(nt(call[...], call[...]) * gram[...], axis=0, keepdims=True)
+        total += jnp.sum(rest, axis=0, keepdims=True)
+        total = jnp.sum(total, axis=1, keepdims=True)
+        total += jnp.sum(jnp.sum(xgram[...], axis=0, keepdims=True), axis=1, keepdims=True)
         nbuf[z] = jnp.broadcast_to(total, (8, 128))
         for k in range(1, NZ):
             send(nbuf.at[z], nbuf.at[z], nsem, k - 1, zdev(k))
@@ -271,20 +276,30 @@
     def norm_wait():
         for k in range(1, NZ):
             arrived(nbuf.at[lax.rem(z + NZ - k, NZ)], nsem, k - 1, zdev(k))
-        sq = jnp.sum(nbuf[...], axis=0)[0:1, 0:1]
+        sq = jnp.sum(nbuf[...], axis=0)
         bound = jnp.sqrt(F32(D * (HQ + KVH) * HD))
-        return bound / jnp.maximum(jnp.sqrt(sq), bound)
+        fbuf[0] = bound / jnp.maximum(jnp.sqrt(sq), bound)
+        send(fbuf.at[0], fbuf.at[1], csem, 6, core)
+
+    def turned_refs(arr, part):
+        hs = h if part == 0 else oh
+        ds = pl.ds(mo(hs * 128, 128), 128)
+        mine, there = ((xt4, xtp), (gt4, gtp))[arr]
+        return mine.at[:, 1 - c, :, ds], there.at[:, :, ds]
+
+    def turned_send(arr, part):
+        src, dst = turned_refs(arr, part)
+        send(src, dst, csem, arr * 2 + part, core)
+
+    def turned_wait(arr, part):
+        arrived(turned_refs(arr, part)[1], csem, arr * 2 + part, core)
 
     def dx_partial(part):
         hs = h if part == 0 else oh
         ds = pl.ds(mo(hs * 128, 128), 128)
-
-        def step(i, carry):
-            cols = pl.ds(mo(i * 512, 512), 512)
-            dxf[ds, cols] = dot(dv[ds, :], wvt[:, cols])
-            return carry
-
-        lax.fori_loop(0, D // 512, step, 0)
+        for i in range(D // 512):
+            cols = slice(i * 512, (i + 1) * 512)
+            dxf[ds, cols] = nt(dv[ds, :], wv[cols, :])
 
     def z_cols(way):
         return pl.ds(0, HALF) if way == 0 else pl.ds(HALF, HALF)
@@ -333,25 +348,13 @@
             total += zr[z_index(part, way, 4)].astype(F32)
         return total.astype(BF16)
 
-    def grad_block(index, factor):
-        ds = pl.ds(mo(index * 288, 16), 288)
-        out = dot(gt[ds, :], call[...]) * factor
-        value = dot(xt[ds, :], dv[...]) * factor
-        return ((0, out[:, :256]), (256, value[:, :128]), (384, out[:, 256:]), (640, value[:, 128:]))
-
-    def core_copy(n):
-        return remote(csend.at[n], crecv.at[n], csem, n, core)
-
-    def core_send(n, factor):
-        for start, piece in grad_block(2 * n + 1 - c, factor):
-            csend[n, :, start:start + piece.shape[1]] = piece.astype(BF16)
-        core_copy(n).start()
-
-    def core_sum(n, factor):
-        core_copy(n).wait()
-        for start, piece in grad_block(2 * n + c, factor):
-            cols = slice(start, start + piece.shape[1])
-            ssum[n, :, cols] = (piece + crecv[n, :, cols].astype(F32)).astype(BF16)
+    def block(n, factor, factorp):
+        out = dot(gt4[n, c], call[...]) * factor + dot(gtp[n], callp[...]) * factorp
+        value = dot(xt4[n, c], dv[...]) * factor + dot(xtp[n], dvp[...]) * factorp
+        ssum[n, :, 0:256] = out[:, :256].astype(BF16)
+        ssum[n, :, 256:384] = value[:, :128].astype(BF16)
+        ssum[n, :, 384:640] = out[:, 256:].astype(BF16)
+        ssum[n, :, 640:768] = value[:, 128:].astype(BF16)
 
     def add(*pieces):
         total = pieces[0].astype(F32)
@@ -375,6 +378,8 @@
         far = yp(2)
         send(ssum.at[2 * far, LOW], a1r.at[0], rsem, 0, ydev(1))
         send(ssum.at[2 * far + 1, LOW], a1r.at[1], rsem, 1, ydev(-1))
+
+    def a_direct():
         send(ssum.at[2 * yp(1) + 1, LOW], a2r.at[0, 1], rsem, 2, ydev(1))
         send(ssum.at[2 * yp(-1), LOW], a2r.at[1, 0], rsem, 3, ydev(-1))
 
@@ -392,38 +397,27 @@
             arrived(a2r.at[way, way], rsem, 4 + way, ydev(1 - 2 * way))
         for ll in range(2):
             ua[ll] = add(ssum[2 * y + ll, LOW, :], a2r[0, ll], a2r[1, ll]).astype(BF16)
-        ph, pll = xhl(2)
-        send(ua.at[pll, pl.ds(0, 80), hcols(ph)], a4r.at[pl.ds(0, 80)], rsem, 6, xdev(1))
-        send(ua.at[pll, pl.ds(80, 64), hcols(ph)], a4r.at[pl.ds(80, 64)], rsem, 7, xdev(-1))
+        for k in range(1, 4):
+            ph, pll = xhl(k)
+            send(ua.at[pll, :, hcols(ph)], a4r.at[k - 1], rsem, 5 + k, xdev(k))
 
     def a_four():
-        for way, (start, size) in enumerate(((0, 80), (80, 64))):
-            step = 1 - 2 * way
-            ds, other = pl.ds(start, size), (pl.ds(80, 64), pl.ds(0, 80))[way]
-            ph, pll = xhl(step)
-            arrived(a4r.at[ds], rsem, 6 + way, xdev(step))
-            a5s[way, ds, :] = add(ua[pll, ds, hcols(ph)], a4r[ds, :]).astype(BF16)
-            a5s[way, other, :] = ua[pll, other, hcols(ph)]
-            send(a5s.at[way], a5r.at[way], rsem, 8 + way, xdev(step))
-
-    def a_five():
-        for way in range(2):
-            arrived(a5r.at[way], rsem, 8 + way, xdev(1 - 2 * way))
-        total = add(ua[l, :, hcols(h)], a5r[0], a5r[1])
+        for k in range(1, 4):
+            arrived(a4r.at[k - 1], rsem, 5 + k, xdev(k))
+        total = add(ua[l, :, hcols(h)], a4r[0], a4r[1], a4r[2])
         outt_ref[0:144, :] = total[:, :256]
         val_ref[0:144, :] = total[:, 256:]
 
     def s_high(yy, ll, hh):
         return ssum.at[2 * yy + ll, HIGH, hcols(hh)]
 
-    def b_one():
+    def b_one(yy, way):
         ph, pll = xhl(2)
-        for yy in range(4):
-            send(s_high(yy, pll, ph), b1r.at[yy], rsem, 10 + yy, xdev(1 if yy < 2 else -1))
-        for yy in range(4):
-            way = 1 if yy < 2 else 0
-            ph, pll = xhl(1 - 2 * way)
-            send(s_high(yy, pll, ph), b2r.at[way, yy], rsem, 14 + yy, xdev(1 - 2 * way))
+        send(s_high(yy, pll, ph), b1r.at[yy], rsem, 10 + yy, xdev(1 - 2 * way))
+
+    def b_direct(yy, way):
+        ph, pll = xhl(1 - 2 * way)
+        send(s_high(yy, pll, ph), b2r.at[way, yy], rsem, 14 + yy, xdev(1 - 2 * way))
 
     def b_two():
         for yy in range(4):
@@ -440,124 +434,139 @@
             arrived(b2r.at[way, yy], rsem, 14 + yy, xdev(1 - 2 * way))
             arrived(b2r.at[1 - way, yy], rsem, 18 + yy, xdev(2 * way - 1))
             ub[yy] = add(ssum[2 * yy + l, HIGH, hcols(h)], b2r[0, yy], b2r[1, yy]).astype(BF16)
-        far = yp(2)
-        send(ub.at[far, pl.ds(0, 80)], b4r.at[pl.ds(0, 80)], rsem, 22, ydev(1))
-        send(ub.at[far, pl.ds(80, 64)], b4r.at[pl.ds(80, 64)], rsem, 23, ydev(-1))
+        for k in range(1, 4):
+            send(ub.at[yp(k)], b4r.at[k - 1], rsem, 21 + k, ydev(k))
 
     def b_four():
-        for way, (start, size) in enumerate(((0, 80), (80, 64))):
-            step = 1 - 2 * way
-            ds, other = pl.ds(start, size), (pl.ds(80, 64), pl.ds(0, 80))[way]
-            arrived(b4r.at[ds], rsem, 22 + way, ydev(step))
-            b5s[way, ds, :] = add(ub[yp(step), ds, :], b4r[ds, :]).astype(BF16)
-            b5s[way, other, :] = ub[yp(step), other, :]
-            send(b5s.at[way], b5r.at[way], rsem, 24 + way, ydev(step))
-
-    def b_five():
-        for way in range(2):
-            arrived(b5r.at[way], rsem, 24 + way, ydev(1 - 2 * way))
-        total = add(ub[y], b5r[0], b5r[1])
+        for k in range(1, 4):
+            arrived(b4r.at[k - 1], rsem, 21 + k, ydev(k))
+        total = add(ub[y], b4r[0], b4r[1], b4r[2])
         outt_ref[144:288, :] = total[:, :256]
         val_ref[144:288, :] = total[:, 256:]
 
-    X, G, OWN, OTHER = 0, 1, 0, 1
-    ex_send(0, x_ref.at[oh])
+    local[1].wait()
+    local[2].wait()
+    softmax(h)
+    pl.semaphore_wait(barrier, len(peers))
+    ex_send(1, gsend)
+    ag_send(G, OWN, 1)
+    w_first(1)
     local[0].wait()
     ag_send(X, OWN, 1)
-    ex_send(1, gsend)
-    ag_send(G, OWN, 1)
-    w_first(0)
+    ag_next(G, OWN, 1)
+    ex_send(0, x_ref.at[oh])
     ex_send(2, q_ref.at[oh])
     ex_send(3, k_ref.at[oh])
-    w_first(1)
-    local[1].wait()
-    local[2].wait()
-    ag_next(X, OWN, 1)
-    ex_wait(0)
-    ag_send(X, OTHER, 1)
-    softmax(h)
-    ag_next(X, OWN, 2)
-    w_second(0)
-    ag_next(X, OTHER, 1)
-    ag_next(G, OWN, 1)
-    ag_next(X, OWN, 3)
-    w_third(0)
-    ag_next(X, OTHER, 2)
+    w_first(0)
     ex_wait(1)
     ag_send(G, OTHER, 1)
+    ag_next(G, OWN, 2)
     w_second(1)
+    ag_next(G, OTHER, 1)
+    ag_next(G, OWN, 3)
     ex_wait(2)
     ex_wait(3)
     softmax(oh)
+    ag_next(X, OWN, 1)
+    w_third(1)
+    ag_next(G, OTHER, 2)
+    w_second(0)
+    ex_wait(0)
+    ag_send(X, OTHER, 1)
+    ag_wait(G, OWN, 4)
+    transpose_half(gall, gt, OWN)
+    turned_send(G, OWN)
+    w_fourth(1)
+    ag_next(G, OTHER, 3)
+    ag_next(X, OWN, 2)
+    w_third(0)
+    w_last(1)
+    local[4].wait()
+    grad_contexts(OWN)
+    ag_next(X, OTHER, 1)
     w_fourth(0)
-    ag_next(X, OTHER, 3)
-    ag_next(G, OWN, 2)
-    ag_wait(X, OWN, 4)
-    transpose_half(xall, xt, OWN)
-    w_third(1)
-    ag_next(G, OTHER, 1)
+    ag_wait(G, OTHER, 4)
+    transpose_half(gall, gt, OTHER)
+    turned_send(G, OTHER)
+    ag_next(X, OWN, 3)
+    grad_contexts(OTHER)
+    grad_values()
+    send(dv, dvp, csem, 4, core)
+    ag_next(X, OTHER, 2)
     w_last(0)
     local[3].wait()
-    values(OWN)
-    ag_next(G, OWN, 3)
-    w_fourth(1)
-    ag_next(G, OTHER, 2)
-    ag_wait(X, OTHER, 4)
-    transpose_half(xall, xt, OTHER)
-    values(OTHER)
-    ag_next(G, OTHER, 3)
-    contexts()
-    wv_turn()
-    w_last(1)
-    local[4].wait()
-    ag_wait(G, OWN, 4)
-    transpose_half(gall, gt, OWN)
-    grad_contexts(OWN)
-    x_gram()
-    ag_wait(G, OTHER, 4)
-    transpose_half(gall, gt, OTHER)
-    grad_contexts(OTHER)
-    grad_values()
     dx_partial(OTHER)
     z_step(OTHER, 1)
+    ag_wait(X, OWN, 4)
+    values(OWN)
+    dx_partial(OWN)
+    ag_next(X, OTHER, 3)
+    z_step(OWN, 1)
+    g_gram()
+    x_gram()
+    transpose_half(xall, xt, OWN)
+    turned_send(X, OWN)
+    ag_wait(X, OTHER, 4)
+    values(OTHER)
+    contexts()
+    send(call, callp, csem, 5, core)
     norm_send()
-    dx_partial(OWN)
-    z_step(OWN, 1)
     z_step(OTHER, 2)
-    factor = norm_wait()
+    transpose_half(xall, xt, OTHER)
+    turned_send(X, OTHER)
     z_step(OWN, 2)
-
-    def first(n, carry):
-        core_send(n, factor)
+    norm_wait()
+    for arr in (G, X):
+        for part in range(2):
+            turned_wait(arr, part)
+    arrived(dvp, csem, 4, core)
+    arrived(callp, csem, 5, core)
+    arrived(fbuf.at[1], csem, 6, core)
+    factor, factorp = fbuf[0][0:1, 0:1], fbuf[1][0:1, 0:1]
+
+    block(2 * yp(2) + l, factor, factorp)
+    block(2 * yp(2) + 1 - l, factor, factorp)
+    a_one()
+
+    def near(yy, carry):
+        block(2 * lax.rem(yy + y + 3, 4) + l, factor, factorp)
         return carry
 
-    def second(n, carry):
-        core_sum(n, factor)
+    lax.fori_loop(0, 3, near, 0)
+    for yy in range(4):
+        b_one(yy, 0 if yy < 2 else 1)
+
+    def rest(yy, carry):
+        block(2 * lax.rem(yy + y + 3, 4) + 1 - l, factor, factorp)
         return carry
 
-    lax.fori_loop(0, 8, first, 0)
+    lax.fori_loop(0, 3, rest, 0)
+    a_direct()
+    for yy in range(4):
+        b_direct(yy, 1 if yy < 2 else 0)
     z_step(OTHER, 3)
-    lax.fori_loop(0, 8, second, 0)
-    a_one()
-    b_one()
     z_step(OWN, 3)
+    z_step(OTHER, 4)
     a_two()
     b_two()
-    z_step(OTHER, 4)
     z_step(OWN, 4)
+    gis[...] = z_final(OTHER)
+    ex_send(4, gis)
+    gi_ref[h] = z_final(OWN)
     a_three()
     b_three()
+    ex_wait(4)
+    gi_ref[oh] = gir[...]
     a_four()
     b_four()
-    gis[...] = z_final(OTHER)
-    ex_send(4, gis)
-    a_five()
-    b_five()
-    gi_ref[h] = z_final(OWN)
-    ex_wait(4)
-    gi_ref[oh] = gir[...]
     for copy in sent:
         copy.wait_send()
+
+
+def finish(outt_ref, val_ref, gi_ref, out_ref, value_ref, grad_ref):
+    out_ref[...] = outt_ref[...].T
+    value_ref[...] = val_ref[...]
+    grad_ref[...] = gi_ref[...]
 
 
 def per_device(layer_input, out_grad, loss_weight, queries, keys, value_weight, output_weight, lengths):
@@ -579,18 +588,16 @@
         in_specs=[smem, smem, any_spec, vmem, any_spec, any_spec, any_spec, any_spec],
         out_specs=(vmem, vmem, vmem),
         scratch_shapes=[
-            buf(SEQ, D), buf(SEQ, D), buf(D, SEQ), buf(D, SEQ), buf(TOK, D),
-            buf(SEQ, 512), buf(SEQ, 256), buf(D, 256), buf(256, D), buf(512, D),
-            buf(4, SEQ, SEQ), buf(SEQ, 256), buf(SEQ, 512), buf(512, SEQ), buf(256, SEQ), buf(SEQ, 256),
-            buf(SEQ, SEQ, dtype=F32), buf(NZ, 8, 128, dtype=F32), buf(SEQ, D, dtype=F32),
-            buf(16, TOK, D), buf(16, TOK, D), buf(TOK, D), buf(TOK, D),
-            buf(8, 288, 768), buf(8, 288, 768), buf(8, 288, 768),
-            buf(2, 144, 768), buf(2, 144, 768), buf(2, 2, 144, 768), buf(2, 144, 768),
-            buf(144, 384), buf(2, 144, 384), buf(2, 144, 384),
-            buf(4, 144, 384), buf(4, 144, 384), buf(2, 4, 144, 384), buf(4, 144, 384),
-            buf(144, 384), buf(2, 144, 384), buf(2, 144, 384),
-            dma((5,)), dma((2, 5)), dma((2, 32)), dma((2, 18)), dma((2, 7)), dma((2, 16)), dma((2, 8)),
-            dma((2, 26)),
+            buf(SEQ, D), buf(SEQ, D), buf(8, 2, 288, SEQ), buf(8, 2, 288, SEQ), buf(8, 288, SEQ), buf(8, 288, SEQ),
+            buf(TOK, D), buf(SEQ, 512), buf(SEQ, 256), buf(D, 256), buf(512, D),
+            buf(4, SEQ, SEQ), buf(SEQ, 256), buf(SEQ, 512), buf(SEQ, 512), buf(512, SEQ), buf(256, SEQ),
+            buf(SEQ, 256), buf(SEQ, 256),
+            buf(SEQ, SEQ, dtype=F32), buf(128, 128, dtype=F32), buf(NZ, 8, 128, dtype=F32), buf(2, 8, 128, dtype=F32),
+            buf(SEQ, D, dtype=F32), buf(16, TOK, D), buf(16, TOK, D), buf(TOK, D), buf(TOK, D), buf(8, 288, 768),
+            buf(2, 144, 768), buf(2, 144, 768), buf(2, 2, 144, 768), buf(2, 144, 768), buf(3, 144, 384),
+            buf(4, 144, 384), buf(4, 144, 384), buf(2, 4, 144, 384), buf(4, 144, 384), buf(3, 144, 384),
+            dma((5,)), dma((2, 5)), dma((2, 32)), dma((2, 18)), dma((2, 7)), dma((2, 16)), dma((2, 7)),
+            dma((2, 25)),
         ],
         compiler_params=pltpu.CompilerParams(
             collective_id=0, has_side_effects=True, vmem_limit_bytes=60 * 1024 * 1024
@@ -598,7 +605,17 @@
         cost_estimate=pl.CostEstimate(flops=5_000_000_000, bytes_accessed=12_000_000, transcendentals=1_000_000),
         name="clipped_grads",
     )(loss_weight, lengths, layer_input, out_grad, queries, keys, value_weight, output_weight)
-    return out_t.T, value, grad_input
+    return pl.pallas_call(
+        finish,
+        out_shape=(
+            jax.ShapeDtypeStruct((256, 288), F32),
+            jax.ShapeDtypeStruct((288, 128), F32),
+            jax.ShapeDtypeStruct((2, TOK, D), BF16),
+        ),
+        in_specs=[vmem] * 3,
+        out_specs=(vmem,) * 3,
+        name="finish",
+    )(out_t, value, grad_input)
 
 
 def solution(mesh):

time: 121 us -> 111 us (0.917); the launches traced: 121 us -> 110 us
  Pallas kernels: 116 us -> 107 us
  local copies, waits for them, and re-layouts: 4.97 us -> 1.85 us
    pallas_call x1, Pallas kernels: 116 us -> 105 us  [per_device(): pl.pallas_call(kernel, out_shape=(jax.ShapeDtypeStruct((288, 256), F32),...]
    unnamed x3 -> x0, local copies, waits for them, and re-layouts: 4.97 us -> none
    pallas_call x0 -> x1, Pallas kernels: none -> 2.1 us  [per_device(): pl.pallas_call(finish, out_shape=(jax.ShapeDtypeStruct((256, 288), F32),...]
    pallas_call x0 -> x1, local copies, waits for them, and re-layouts: none -> 1.85 us  [per_device(): pl.pallas_call(finish, out_shape=(jax.ShapeDtypeStruct((256, 288), F32),...]
where the time goes in v2:
time: 111 us; the launch traced here: 110 us
  Pallas kernels  107 us (96%)
  local copies, waits for them, and re-layouts  1.85 us (2%)
    pallas_call x1, Pallas kernels, per_device(): pl.pallas_call(kernel, out_shape=(jax.ShapeDtypeStruct((288, 256), F32),...  105 us

profile of v2, /device:TPU:1, one launch (start us, length us, event | category | flops | bytes accessed | tf_op | source)
XLA Modules:
  0.0 109.7 jit_solution(323352253352609079)
XLA Ops:
  0.6 105.1 %clipped_grads.1 = (f32[288,256]{1,0:T(8,128)}, f32[288,128]{1,0:T(8,128)}, bf16[2,16,4608]{2,1,0:T(8,128)(2,1)}) custom-call(f32[2]{0:T(128)} %lw_ref.1, s32[2]{0:T(128)} %len_ref.1, bf16[2,16,4608]{2,1,0:T(8,128)(2,1)} %x_ref.1, bf16[2,16,4608]{2,1,0:T(8,128)(2,1)} %g_ref.1, bf16[2,256,256]{2,1,0:T(8,128)(2,1)} %q_ref.1, bf16[2,256,128]{2,1,0:T(8,128)(2,1)} %k_ref.1, ...), custom_call_target="tpu_custom_call" | custom-call | flops 5000000000 | bytes 12000000 | tf_op jit(solution)/shard_map/clipped_grads/pallas_call | solution.py:581
  105.7 2.1 %finish.1 = (f32[256,288]{1,0:T(8,128)}, f32[288,128]{1,0:T(8,128)}, bf16[2,16,4608]{2,1,0:T(8,128)(2,1)}) custom-call(f32[288,256]{1,0:T(8,128)} %get-tuple-element.6.outt_ref, f32[288,128]{1,0:T(8,128)} %get-tuple-element.7.val_ref, bf16[2,16,4608]{2,1,0:T(8,128)(2,1)} %get-tuple-element.8.gi_ref), custom_call_target="tpu_custom_call" | custom-call | tf_op jit(solution)/shard_map/finish/pallas_call | solution.py:608
  107.8 1.9 %copy.11 = f32[256,288]{0,1:T(8,128)} copy(f32[256,288]{1,0:T(8,128)} %get-tuple-element.9) | data formatting | bytes 589824 | tf_op jit(solution)/shard_map/finish/pallas_call | solution.py:608

commit v3 on v2

--- a/solution.py
+++ b/solution.py
@@ -32,7 +32,7 @@
     lw_ref, len_ref, x_ref, g_ref, q_ref, k_ref, wv_ref, wo_ref,
     outt_ref, val_ref, gi_ref,
     xall, gall, xt4, gt4, xtp, gtp, gsend, qall, kall, wv, wo, probs, vall, call, callp, dct, dvt, dv, dvp,
-    gram, xgram, nbuf, fbuf, dxf, zs, zr, gis, gir, ssum,
+    gram, xgram, nbuf, dxf, zs, zr, gis, gir, ssum,
     a1r, a2s, a2r, ua, a4r, b1r, b2s, b2r, ub, b4r,
     lsem, xsem, agsem, wsem, nsem, zsem, csem, rsem,
 ):
@@ -269,17 +269,25 @@
         total += jnp.sum(rest, axis=0, keepdims=True)
         total = jnp.sum(total, axis=1, keepdims=True)
         total += jnp.sum(jnp.sum(xgram[...], axis=0, keepdims=True), axis=1, keepdims=True)
-        nbuf[z] = jnp.broadcast_to(total, (8, 128))
+        nbuf[c, z] = jnp.broadcast_to(total, (8, 128))
+        mine = nbuf.at[c, z]
+        send(mine, mine, nsem, 0, core)
         for k in range(1, NZ):
-            send(nbuf.at[z], nbuf.at[z], nsem, k - 1, zdev(k))
+            send(mine, mine, nsem, 2 * k - 1, zdev(k))
+            send(mine, mine, nsem, 2 * k, (dp + 1 - 2 * c, zdev(k)[1]))
 
     def norm_wait():
+        arrived(nbuf.at[1 - c, z], nsem, 0, core)
         for k in range(1, NZ):
-            arrived(nbuf.at[lax.rem(z + NZ - k, NZ)], nsem, k - 1, zdev(k))
-        sq = jnp.sum(nbuf[...], axis=0)
+            origin = lax.rem(z + NZ - k, NZ)
+            arrived(nbuf.at[c, origin], nsem, 2 * k - 1, zdev(k))
+            arrived(nbuf.at[1 - c, origin], nsem, 2 * k, (dp + 1 - 2 * c, zdev(k)[1]))
         bound = jnp.sqrt(F32(D * (HQ + KVH) * HD))
-        fbuf[0] = bound / jnp.maximum(jnp.sqrt(sq), bound)
-        send(fbuf.at[0], fbuf.at[1], csem, 6, core)
+        factors = []
+        for cc in (c, 1 - c):
+            sq = jnp.sum(nbuf[cc], axis=0)[0:1, 0:1]
+            factors.append(bound / jnp.maximum(jnp.sqrt(sq), bound))
+        return factors
 
     def turned_refs(arr, part):
         hs = h if part == 0 else oh
@@ -348,13 +356,14 @@
             total += zr[z_index(part, way, 4)].astype(F32)
         return total.astype(BF16)
 
-    def block(n, factor, factorp):
+    def block(yy, ll, factor, factorp):
+        n = 2 * yy + ll
         out = dot(gt4[n, c], call[...]) * factor + dot(gtp[n], callp[...]) * factorp
         value = dot(xt4[n, c], dv[...]) * factor + dot(xtp[n], dvp[...]) * factorp
-        ssum[n, :, 0:256] = out[:, :256].astype(BF16)
-        ssum[n, :, 256:384] = value[:, :128].astype(BF16)
-        ssum[n, :, 384:640] = out[:, 256:].astype(BF16)
-        ssum[n, :, 640:768] = value[:, 128:].astype(BF16)
+        ssum[ll, yy, :, 0:256] = out[:, :256].astype(BF16)
+        ssum[ll, yy, :, 256:384] = value[:, :128].astype(BF16)
+        ssum[ll, yy, :, 384:640] = out[:, 256:].astype(BF16)
+        ssum[ll, yy, :, 640:768] = value[:, 128:].astype(BF16)
 
     def add(*pieces):
         total = pieces[0].astype(F32)
@@ -362,8 +371,6 @@
             total += piece.astype(F32)
         return total
 
-    LOW, HIGH = pl.ds(0, 144), pl.ds(144, 144)
-
     def yp(step):
         return lax.rem(y + step + 4, 4)
 
@@ -374,75 +381,90 @@
         there = xpos(step)
         return lax.div(there, 2), lax.rem(there, 2)
 
-    def a_one():
+    parts = (pl.ds(0, 80), pl.ds(80, 64))
+    highs = (pl.ds(144, 80), pl.ds(224, 64))
+
+    def a_one(q):
         far = yp(2)
-        send(ssum.at[2 * far, LOW], a1r.at[0], rsem, 0, ydev(1))
-        send(ssum.at[2 * far + 1, LOW], a1r.at[1], rsem, 1, ydev(-1))
-
-    def a_direct():
-        send(ssum.at[2 * yp(1) + 1, LOW], a2r.at[0, 1], rsem, 2, ydev(1))
-        send(ssum.at[2 * yp(-1), LOW], a2r.at[1, 0], rsem, 3, ydev(-1))
-
-    def a_two():
+        ds = parts[q]
+        send(ssum.at[0, far, ds], a1r.at[0, ds], rsem, 25 * q, ydev(1))
+        send(ssum.at[1, far, ds], a1r.at[1, ds], rsem, 25 * q + 1, ydev(-1))
+
+    def a_direct(q):
+        ds = parts[q]
+        send(ssum.at[1, yp(1), ds], a2r.at[0, 1, ds], rsem, 25 * q + 2, ydev(1))
+        send(ssum.at[0, yp(-1), ds], a2r.at[1, 0, ds], rsem, 25 * q + 3, ydev(-1))
+
+    def a_two(q):
+        ds = parts[q]
         for way in range(2):
             step = 1 - 2 * way
-            arrived(a1r.at[way], rsem, way, ydev(step))
-            a2s[way] = add(ssum[2 * yp(step) + way, LOW, :], a1r[way]).astype(BF16)
-            send(a2s.at[way], a2r.at[way, way], rsem, 4 + way, ydev(step))
-
-    def a_three():
-        arrived(a2r.at[0, 1], rsem, 2, ydev(1))
-        arrived(a2r.at[1, 0], rsem, 3, ydev(-1))
-        for way in range(2):
-            arrived(a2r.at[way, way], rsem, 4 + way, ydev(1 - 2 * way))
+            arrived(a1r.at[way, ds], rsem, 25 * q + way, ydev(step))
+            a2s[way, ds, :] = add(ssum[way, yp(step), ds, :], a1r[way, ds, :]).astype(BF16)
+            send(a2s.at[way, ds], a2r.at[way, way, ds], rsem, 25 * q + 4 + way, ydev(step))
+
+    def a_three(q):
+        ds = parts[q]
+        arrived(a2r.at[0, 1, ds], rsem, 25 * q + 2, ydev(1))
+        arrived(a2r.at[1, 0, ds], rsem, 25 * q + 3, ydev(-1))
+        for way in range(2):
+            arrived(a2r.at[way, way, ds], rsem, 25 * q + 4 + way, ydev(1 - 2 * way))
         for ll in range(2):
-            ua[ll] = add(ssum[2 * y + ll, LOW, :], a2r[0, ll], a2r[1, ll]).astype(BF16)
+            ua[ll, ds, :] = add(ssum[ll, y, ds, :], a2r[0, ll, ds, :], a2r[1, ll, ds, :]).astype(BF16)
         for k in range(1, 4):
             ph, pll = xhl(k)
-            send(ua.at[pll, :, hcols(ph)], a4r.at[k - 1], rsem, 5 + k, xdev(k))
-
-    def a_four():
+            send(ua.at[pll, ds, hcols(ph)], a4r.at[k - 1, ds], rsem, 25 * q + 5 + k, xdev(k))
+
+    def a_four(q):
+        ds = parts[q]
         for k in range(1, 4):
-            arrived(a4r.at[k - 1], rsem, 5 + k, xdev(k))
-        total = add(ua[l, :, hcols(h)], a4r[0], a4r[1], a4r[2])
-        outt_ref[0:144, :] = total[:, :256]
-        val_ref[0:144, :] = total[:, 256:]
-
-    def s_high(yy, ll, hh):
-        return ssum.at[2 * yy + ll, HIGH, hcols(hh)]
-
-    def b_one(yy, way):
+            arrived(a4r.at[k - 1, ds], rsem, 25 * q + 5 + k, xdev(k))
+        total = add(ua[l, ds, hcols(h)], a4r[0, ds, :], a4r[1, ds, :], a4r[2, ds, :])
+        outt_ref[ds, :] = total[:, :256]
+        val_ref[ds, :] = total[:, 256:]
+
+    pairs = (pl.ds(0, 2), pl.ds(2, 2))
+
+    def s_high(q, pair, ll, hh):
+        return ssum.at[ll, pairs[pair], highs[q], hcols(hh)]
+
+    def b_one(q):
         ph, pll = xhl(2)
-        send(s_high(yy, pll, ph), b1r.at[yy], rsem, 10 + yy, xdev(1 - 2 * way))
-
-    def b_direct(yy, way):
-        ph, pll = xhl(1 - 2 * way)
-        send(s_high(yy, pll, ph), b2r.at[way, yy], rsem, 14 + yy, xdev(1 - 2 * way))
-
-    def b_two():
-        for yy in range(4):
-            way = 0 if yy < 2 else 1
+        for way in range(2):
+            send(s_high(q, way, pll, ph), b1r.at[pairs[way], parts[q]], rsem, 25 * q + 10 + way, xdev(1 - 2 * way))
+
+    def b_direct(q):
+        for way in range(2):
+            ph, pll = xhl(1 - 2 * way)
+            send(s_high(q, 1 - way, pll, ph), b2r.at[way, pairs[1 - way], parts[q]], rsem, 25 * q + 14 + way, xdev(1 - 2 * way))
+
+    def b_two(q):
+        ds = parts[q]
+        for way in range(2):
             step = 1 - 2 * way
             ph, pll = xhl(step)
-            arrived(b1r.at[yy], rsem, 10 + yy, xdev(step))
-            b2s[yy] = add(ssum[2 * yy + pll, HIGH, hcols(ph)], b1r[yy]).astype(BF16)
-            send(b2s.at[yy], b2r.at[way, yy], rsem, 18 + yy, xdev(step))
-
-    def b_three():
+            arrived(b1r.at[pairs[way], ds], rsem, 25 * q + 10 + way, xdev(step))
+            for yy in (2 * way, 2 * way + 1):
+                b2s[yy, ds, :] = add(ssum[pll, yy, highs[q], hcols(ph)], b1r[yy, ds, :]).astype(BF16)
+            send(b2s.at[pairs[way], ds], b2r.at[way, pairs[way], ds], rsem, 25 * q + 18 + way, xdev(step))
+
+    def b_three(q):
+        ds = parts[q]
+        for way in range(2):
+            arrived(b2r.at[way, pairs[1 - way], ds], rsem, 25 * q + 14 + way, xdev(1 - 2 * way))
+            arrived(b2r.at[way, pairs[way], ds], rsem, 25 * q + 18 + way, xdev(1 - 2 * way))
         for yy in range(4):
-            way = 1 if yy < 2 else 0
-            arrived(b2r.at[way, yy], rsem, 14 + yy, xdev(1 - 2 * way))
-            arrived(b2r.at[1 - way, yy], rsem, 18 + yy, xdev(2 * way - 1))
-            ub[yy] = add(ssum[2 * yy + l, HIGH, hcols(h)], b2r[0, yy], b2r[1, yy]).astype(BF16)
+            ub[yy, ds, :] = add(ssum[l, yy, highs[q], hcols(h)], b2r[0, yy, ds, :], b2r[1, yy, ds, :]).astype(BF16)
         for k in range(1, 4):
-            send(ub.at[yp(k)], b4r.at[k - 1], rsem, 21 + k, ydev(k))
-
-    def b_four():
+            send(ub.at[yp(k), ds], b4r.at[k - 1, ds], rsem, 25 * q + 21 + k, ydev(k))
+
+    def b_four(q):
+        ds = parts[q]
         for k in range(1, 4):
-            arrived(b4r.at[k - 1], rsem, 21 + k, ydev(k))
-        total = add(ub[y], b4r[0], b4r[1], b4r[2])
-        outt_ref[144:288, :] = total[:, :256]
-        val_ref[144:288, :] = total[:, 256:]
+            arrived(b4r.at[k - 1, ds], rsem, 25 * q + 21 + k, ydev(k))
+        total = add(ub[y, ds, :], b4r[0, ds, :], b4r[1, ds, :], b4r[2, ds, :])
+        outt_ref[highs[q], :] = total[:, :256]
+        val_ref[highs[q], :] = total[:, 256:]
 
     local[1].wait()
     local[2].wait()
@@ -455,42 +477,42 @@
     ag_send(X, OWN, 1)
     ag_next(G, OWN, 1)
     ex_send(0, x_ref.at[oh])
-    ex_send(2, q_ref.at[oh])
-    ex_send(3, k_ref.at[oh])
-    w_first(0)
     ex_wait(1)
     ag_send(G, OTHER, 1)
     ag_next(G, OWN, 2)
     w_second(1)
     ag_next(G, OTHER, 1)
+    w_first(0)
     ag_next(G, OWN, 3)
-    ex_wait(2)
-    ex_wait(3)
-    softmax(oh)
     ag_next(X, OWN, 1)
     w_third(1)
     ag_next(G, OTHER, 2)
-    w_second(0)
     ex_wait(0)
     ag_send(X, OTHER, 1)
+    ex_send(2, q_ref.at[oh])
+    ex_send(3, k_ref.at[oh])
     ag_wait(G, OWN, 4)
     transpose_half(gall, gt, OWN)
     turned_send(G, OWN)
     w_fourth(1)
+    w_second(0)
     ag_next(G, OTHER, 3)
     ag_next(X, OWN, 2)
-    w_third(0)
     w_last(1)
     local[4].wait()
     grad_contexts(OWN)
     ag_next(X, OTHER, 1)
-    w_fourth(0)
+    w_third(0)
+    ex_wait(2)
+    ex_wait(3)
+    softmax(oh)
     ag_wait(G, OTHER, 4)
     transpose_half(gall, gt, OTHER)
     turned_send(G, OTHER)
     ag_next(X, OWN, 3)
     grad_contexts(OTHER)
     grad_values()
+    w_fourth(0)
     send(dv, dvp, csem, 4, core)
     ag_next(X, OTHER, 2)
     w_last(0)
@@ -506,65 +528,72 @@
     x_gram()
     transpose_half(xall, xt, OWN)
     turned_send(X, OWN)
+    for part in range(2):
+        turned_wait(G, part)
+    z_step(OTHER, 2)
     ag_wait(X, OTHER, 4)
     values(OTHER)
     contexts()
     send(call, callp, csem, 5, core)
     norm_send()
-    z_step(OTHER, 2)
     transpose_half(xall, xt, OTHER)
     turned_send(X, OTHER)
     z_step(OWN, 2)
-    norm_wait()
-    for arr in (G, X):
-        for part in range(2):
-            turned_wait(arr, part)
     arrived(dvp, csem, 4, core)
     arrived(callp, csem, 5, core)
-    arrived(fbuf.at[1], csem, 6, core)
-    factor, factorp = fbuf[0][0:1, 0:1], fbuf[1][0:1, 0:1]
-
-    block(2 * yp(2) + l, factor, factorp)
-    block(2 * yp(2) + 1 - l, factor, factorp)
-    a_one()
+    for part in range(2):
+        turned_wait(X, part)
+    z_step(OTHER, 3)
+    factor, factorp = norm_wait()
+
+    block(yp(2), l, factor, factorp)
+    block(yp(2), 1 - l, factor, factorp)
+    a_one(0)
+    a_one(1)
 
     def near(yy, carry):
-        block(2 * lax.rem(yy + y + 3, 4) + l, factor, factorp)
+        block(lax.rem(yy + y + 3, 4), l, factor, factorp)
         return carry
 
     lax.fori_loop(0, 3, near, 0)
-    for yy in range(4):
-        b_one(yy, 0 if yy < 2 else 1)
+    b_one(0)
+    b_one(1)
 
     def rest(yy, carry):
-        block(2 * lax.rem(yy + y + 3, 4) + 1 - l, factor, factorp)
+        block(lax.rem(yy + y + 3, 4), 1 - l, factor, factorp)
         return carry
 
     lax.fori_loop(0, 3, rest, 0)
-    a_direct()
-    for yy in range(4):
-        b_direct(yy, 1 if yy < 2 else 0)
-    z_step(OTHER, 3)
+    a_direct(0)
+    b_direct(0)
     z_step(OWN, 3)
     z_step(OTHER, 4)
-    a_two()
-    b_two()
+    a_two(0)
+    a_direct(1)
+    b_two(0)
+    b_direct(1)
+    a_two(1)
+    b_two(1)
     z_step(OWN, 4)
     gis[...] = z_final(OTHER)
     ex_send(4, gis)
+    a_three(0)
+    b_three(0)
     gi_ref[h] = z_final(OWN)
-    a_three()
-    b_three()
+    a_three(1)
+    b_three(1)
+    a_four(0)
+    b_four(0)
     ex_wait(4)
     gi_ref[oh] = gir[...]
-    a_four()
-    b_four()
+    a_four(1)
+    b_four(1)
     for copy in sent:
         copy.wait_send()
 
 
 def finish(outt_ref, val_ref, gi_ref, out_ref, value_ref, grad_ref):
-    out_ref[...] = outt_ref[...].T
+    out_ref[...] = outt_ref[...]
     value_ref[...] = val_ref[...]
     grad_ref[...] = gi_ref[...]
 
@@ -592,12 +621,12 @@
             buf(TOK, D), buf(SEQ, 512), buf(SEQ, 256), buf(D, 256), buf(512, D),
             buf(4, SEQ, SEQ), buf(SEQ, 256), buf(SEQ, 512), buf(SEQ, 512), buf(512, SEQ), buf(256, SEQ),
             buf(SEQ, 256), buf(SEQ, 256),
-            buf(SEQ, SEQ, dtype=F32), buf(128, 128, dtype=F32), buf(NZ, 8, 128, dtype=F32), buf(2, 8, 128, dtype=F32),
-            buf(SEQ, D, dtype=F32), buf(16, TOK, D), buf(16, TOK, D), buf(TOK, D), buf(TOK, D), buf(8, 288, 768),
+            buf(SEQ, SEQ, dtype=F32), buf(128, 128, dtype=F32), buf(2, NZ, 8, 128, dtype=F32),
+            buf(SEQ, D, dtype=F32), buf(16, TOK, D), buf(16, TOK, D), buf(TOK, D), buf(TOK, D), buf(2, 4, 288, 768),
             buf(2, 144, 768), buf(2, 144, 768), buf(2, 2, 144, 768), buf(2, 144, 768), buf(3, 144, 384),
             buf(4, 144, 384), buf(4, 144, 384), buf(2, 4, 144, 384), buf(4, 144, 384), buf(3, 144, 384),
-            dma((5,)), dma((2, 5)), dma((2, 32)), dma((2, 18)), dma((2, 7)), dma((2, 16)), dma((2, 7)),
-            dma((2, 25)),
+            dma((5,)), dma((2, 5)), dma((2, 32)), dma((2, 18)), dma((2, 15)), dma((2, 16)), dma((2, 6)),
+            dma((2, 50)),
         ],
         compiler_params=pltpu.CompilerParams(
             collective_id=0, has_side_effects=True, vmem_limit_bytes=60 * 1024 * 1024
@@ -605,17 +634,19 @@
         cost_estimate=pl.CostEstimate(flops=5_000_000_000, bytes_accessed=12_000_000, transcendentals=1_000_000),
         name="clipped_grads",
     )(loss_weight, lengths, layer_input, out_grad, queries, keys, value_weight, output_weight)
-    return pl.pallas_call(
+    out_t, value, grad_input = pl.pallas_call(
         finish,
         out_shape=(
-            jax.ShapeDtypeStruct((256, 288), F32),
+            jax.ShapeDtypeStruct((288, 256), F32),
             jax.ShapeDtypeStruct((288, 128), F32),
             jax.ShapeDtypeStruct((2, TOK, D), BF16),
         ),
         in_specs=[vmem] * 3,
         out_specs=(vmem,) * 3,
+        compiler_params=pltpu.CompilerParams(vmem_limit_bytes=60 * 1024 * 1024),
         name="finish",
     )(out_t, value, grad_input)
+    return out_t.T, value, grad_input
 
 
 def solution(mesh):

time: 111 us -> 103 us (0.928)
  Pallas kernels: 107 us -> 101 us
  local copies, waits for them, and re-layouts: 1.85 us -> 0 us
    pallas_call x1, Pallas kernels: 105 us -> 98.8 us  [per_device(): pl.pallas_call(kernel, out_shape=(jax.ShapeDtypeStruct((288, 256), F32),...]
    pallas_call x1 -> x0, local copies, waits for them, and re-layouts: 1.85 us -> none  [per_device(): pl.pallas_call(finish, out_shape=(jax.ShapeDtypeStruct((256, 288), F32),...]
where the time goes in v3:
time: 103 us; the launch traced here: 101 us
  Pallas kernels  101 us (98%)
    pallas_call x1, Pallas kernels, per_device(): pl.pallas_call(kernel, out_shape=(jax.ShapeDtypeStruct((288, 256), F32),...  98.8 us

profile of v3, /device:TPU:1, one launch (start us, length us, event | category | flops | bytes accessed | tf_op | source)
XLA Modules:
  0.0 101.5 jit_solution(12411440515758634928)
XLA Ops:
  0.6 98.8 %clipped_grads.1 = (f32[288,256]{1,0:T(8,128)}, f32[288,128]{1,0:T(8,128)}, bf16[2,16,4608]{2,1,0:T(8,128)(2,1)}) custom-call(f32[2]{0:T(128)} %lw_ref.1, s32[2]{0:T(128)} %len_ref.1, bf16[2,16,4608]{2,1,0:T(8,128)(2,1)} %x_ref.1, bf16[2,16,4608]{2,1,0:T(8,128)(2,1)} %g_ref.1, bf16[2,256,256]{2,1,0:T(8,128)(2,1)} %q_ref.1, bf16[2,256,128]{2,1,0:T(8,128)(2,1)} %k_ref.1, ...), custom_call_target="tpu_custom_call" | custom-call | flops 5000000000 | bytes 12000000 | tf_op jit(solution)/shard_map/clipped_grads/pallas_call | solution.py:610
  99.5 2.0 %finish.1 = (f32[288,256]{1,0:T(8,128)}, f32[288,128]{1,0:T(8,128)}, bf16[2,16,4608]{2,1,0:T(8,128)(2,1)}) custom-call(f32[288,256]{1,0:T(8,128)} %get-tuple-element.9.outt_ref, f32[288,128]{1,0:T(8,128)} %get-tuple-element.10.val_ref, bf16[2,16,4608]{2,1,0:T(8,128)(2,1)} %get-tuple-element.11.gi_ref), custom_call_target="tpu_custom_call" | custom-call | tf_op jit(solution)/shard_map/finish/pallas_call | solution.py:637

commit v4 on v3

--- a/solution.py
+++ b/solution.py
@@ -269,10 +269,10 @@
         total += jnp.sum(rest, axis=0, keepdims=True)
         total = jnp.sum(total, axis=1, keepdims=True)
         total += jnp.sum(jnp.sum(xgram[...], axis=0, keepdims=True), axis=1, keepdims=True)
-        nbuf[c, z] = jnp.broadcast_to(total, (8, 128))
+        nbuf[c, z] = jnp.broadcast_to(total, (1, 128))
         mine = nbuf.at[c, z]
         send(mine, mine, nsem, 0, core)
-        for k in range(1, NZ):
+        for k in (4, 3, 5, 2, 6, 1, 7):
             send(mine, mine, nsem, 2 * k - 1, zdev(k))
             send(mine, mine, nsem, 2 * k, (dp + 1 - 2 * c, zdev(k)[1]))
 
@@ -381,8 +381,9 @@
         there = xpos(step)
         return lax.div(there, 2), lax.rem(there, 2)
 
-    parts = (pl.ds(0, 80), pl.ds(80, 64))
-    highs = (pl.ds(144, 80), pl.ds(224, 64))
+    parts = (pl.ds(0, 80), pl.ds(80, 80))
+    bparts = (pl.ds(0, 64), pl.ds(64, 64))
+    highs = (pl.ds(160, 64), pl.ds(224, 64))
 
     def a_one(q):
         far = yp(2)
@@ -431,15 +432,15 @@
     def b_one(q):
         ph, pll = xhl(2)
         for way in range(2):
-            send(s_high(q, way, pll, ph), b1r.at[pairs[way], parts[q]], rsem, 25 * q + 10 + way, xdev(1 - 2 * way))
+            send(s_high(q, way, pll, ph), b1r.at[pairs[way], bparts[q]], rsem, 25 * q + 10 + way, xdev(1 - 2 * way))
 
     def b_direct(q):
         for way in range(2):
             ph, pll = xhl(1 - 2 * way)
-            send(s_high(q, 1 - way, pll, ph), b2r.at[way, pairs[1 - way], parts[q]], rsem, 25 * q + 14 + way, xdev(1 - 2 * way))
+            send(s_high(q, 1 - way, pll, ph), b2r.at[way, pairs[1 - way], bparts[q]], rsem, 25 * q + 14 + way, xdev(1 - 2 * way))
 
     def b_two(q):
-        ds = parts[q]
+        ds = bparts[q]
         for way in range(2):
             step = 1 - 2 * way
             ph, pll = xhl(step)
@@ -449,7 +450,7 @@
             send(b2s.at[pairs[way], ds], b2r.at[way, pairs[way], ds], rsem, 25 * q + 18 + way, xdev(step))
 
     def b_three(q):
-        ds = parts[q]
+        ds = bparts[q]
         for way in range(2):
             arrived(b2r.at[way, pairs[1 - way], ds], rsem, 25 * q + 14 + way, xdev(1 - 2 * way))
             arrived(b2r.at[way, pairs[way], ds], rsem, 25 * q + 18 + way, xdev(1 - 2 * way))
@@ -459,7 +460,7 @@
             send(ub.at[yp(k), ds], b4r.at[k - 1, ds], rsem, 25 * q + 21 + k, ydev(k))
 
     def b_four(q):
-        ds = parts[q]
+        ds = bparts[q]
         for k in range(1, 4):
             arrived(b4r.at[k - 1, ds], rsem, 25 * q + 21 + k, ydev(k))
         total = add(ub[y, ds, :], b4r[0, ds, :], b4r[1, ds, :], b4r[2, ds, :])
@@ -518,11 +519,11 @@
     w_last(0)
     local[3].wait()
     dx_partial(OTHER)
-    z_step(OTHER, 1)
     ag_wait(X, OWN, 4)
     values(OWN)
     dx_partial(OWN)
     ag_next(X, OTHER, 3)
+    z_step(OTHER, 1)
     z_step(OWN, 1)
     g_gram()
     x_gram()
@@ -530,12 +531,12 @@
     turned_send(X, OWN)
     for part in range(2):
         turned_wait(G, part)
-    z_step(OTHER, 2)
     ag_wait(X, OTHER, 4)
     values(OTHER)
     contexts()
     send(call, callp, csem, 5, core)
     norm_send()
+    z_step(OTHER, 2)
     transpose_half(xall, xt, OTHER)
     turned_send(X, OTHER)
     z_step(OWN, 2)
@@ -567,21 +568,21 @@
     a_direct(0)
     b_direct(0)
     z_step(OWN, 3)
-    z_step(OTHER, 4)
     a_two(0)
     a_direct(1)
     b_two(0)
     b_direct(1)
+    z_step(OTHER, 4)
     a_two(1)
     b_two(1)
+    a_three(0)
+    b_three(0)
     z_step(OWN, 4)
     gis[...] = z_final(OTHER)
     ex_send(4, gis)
-    a_three(0)
-    b_three(0)
-    gi_ref[h] = z_final(OWN)
     a_three(1)
     b_three(1)
+    gi_ref[h] = z_final(OWN)
     a_four(0)
     b_four(0)
     ex_wait(4)
@@ -621,10 +622,10 @@
             buf(TOK, D), buf(SEQ, 512), buf(SEQ, 256), buf(D, 256), buf(512, D),
             buf(4, SEQ, SEQ), buf(SEQ, 256), buf(SEQ, 512), buf(SEQ, 512), buf(512, SEQ), buf(256, SEQ),
             buf(SEQ, 256), buf(SEQ, 256),
-            buf(SEQ, SEQ, dtype=F32), buf(128, 128, dtype=F32), buf(2, NZ, 8, 128, dtype=F32),
+            buf(SEQ, SEQ, dtype=F32), buf(128, 128, dtype=F32), buf(2, NZ, 1, 128, dtype=F32),
             buf(SEQ, D, dtype=F32), buf(16, TOK, D), buf(16, TOK, D), buf(TOK, D), buf(TOK, D), buf(2, 4, 288, 768),
-            buf(2, 144, 768), buf(2, 144, 768), buf(2, 2, 144, 768), buf(2, 144, 768), buf(3, 144, 384),
-            buf(4, 144, 384), buf(4, 144, 384), buf(2, 4, 144, 384), buf(4, 144, 384), buf(3, 144, 384),
+            buf(2, 160, 768), buf(2, 160, 768), buf(2, 2, 160, 768), buf(2, 160, 768), buf(3, 160, 384),
+            buf(4, 128, 384), buf(4, 128, 384), buf(2, 4, 128, 384), buf(4, 128, 384), buf(3, 128, 384),
             dma((5,)), dma((2, 5)), dma((2, 32)), dma((2, 18)), dma((2, 15)), dma((2, 16)), dma((2, 6)),
             dma((2, 50)),
         ],

time: 103 us -> 97.9 us (0.950); the launches traced: 101 us -> 97.8 us
  Pallas kernels: 101 us -> 97.1 us
    pallas_call x1, Pallas kernels: 98.8 us -> 95.1 us  [per_device(): pl.pallas_call(kernel, out_shape=(jax.ShapeDtypeStruct((288, 256), F32),...]
where the time goes in v4:
time: 97.9 us; the launch traced here: 97.8 us
  Pallas kernels  97.1 us (99%)
    pallas_call x1, Pallas kernels, per_device(): pl.pallas_call(kernel, out_shape=(jax.ShapeDtypeStruct((288, 256), F32),...  95.1 us
    pallas_call x1, Pallas kernels, per_device(): pl.pallas_call(finish, out_shape=(jax.ShapeDtypeStruct((288, 256), F32),...  2 us

profile of v4, /device:TPU:1, one launch (start us, length us, event | category | flops | bytes accessed | tf_op | source)
XLA Modules:
  0.0 97.8 jit_solution(12202115316940367483)
XLA Ops:
  0.6 95.1 %clipped_grads.1 = (f32[288,256]{1,0:T(8,128)}, f32[288,128]{1,0:T(8,128)}, bf16[2,16,4608]{2,1,0:T(8,128)(2,1)}) custom-call(f32[2]{0:T(128)} %lw_ref.1, s32[2]{0:T(128)} %len_ref.1, bf16[2,16,4608]{2,1,0:T(8,128)(2,1)} %x_ref.1, bf16[2,16,4608]{2,1,0:T(8,128)(2,1)} %g_ref.1, bf16[2,256,256]{2,1,0:T(8,128)(2,1)} %q_ref.1, bf16[2,256,128]{2,1,0:T(8,128)(2,1)} %k_ref.1, ...), custom_call_target="tpu_custom_call" | custom-call | flops 5000000000 | bytes 12000000 | tf_op jit(solution)/shard_map/clipped_grads/pallas_call | solution.py:611
  95.8 2.0 %finish.1 = (f32[288,256]{1,0:T(8,128)}, f32[288,128]{1,0:T(8,128)}, bf16[2,16,4608]{2,1,0:T(8,128)(2,1)}) custom-call(f32[288,256]{1,0:T(8,128)} %get-tuple-element.9.outt_ref, f32[288,128]{1,0:T(8,128)} %get-tuple-element.10.val_ref, bf16[2,16,4608]{2,1,0:T(8,128)(2,1)} %get-tuple-element.11.gi_ref), custom_call_target="tpu_custom_call" | custom-call | tf_op jit(solution)/shard_map/finish/pallas_call | solution.py:638

commit v5 on v4

--- a/solution.py
+++ b/solution.py
@@ -75,6 +75,11 @@
         copy = remote(src, dst, sem, index, device)
         copy.start()
         sent.append(copy)
+
+    def drain(count):
+        for copy in sent[:count]:
+            copy.wait_send()
+        del sent[:count]
 
     def arrived(dst, sem, index, device):
         remote(dst, dst, sem, index, device).wait_recv()
@@ -507,6 +512,7 @@
     ex_wait(2)
     ex_wait(3)
     softmax(oh)
+    early = len(sent)
     ag_wait(G, OTHER, 4)
     transpose_half(gall, gt, OTHER)
     turned_send(G, OTHER)
@@ -531,11 +537,13 @@
     turned_send(X, OWN)
     for part in range(2):
         turned_wait(G, part)
+    drain(early)
     ag_wait(X, OTHER, 4)
+    gathers = len(sent)
     values(OTHER)
     contexts()
+    norm_send()
     send(call, callp, csem, 5, core)
-    norm_send()
     z_step(OTHER, 2)
     transpose_half(xall, xt, OTHER)
     turned_send(X, OTHER)
@@ -545,6 +553,8 @@
     for part in range(2):
         turned_wait(X, part)
     z_step(OTHER, 3)
+    drain(gathers)
+    before = len(sent)
     factor, factorp = norm_wait()
 
     block(yp(2), l, factor, factorp)
@@ -556,7 +566,7 @@
         block(lax.rem(yy + y + 3, 4), l, factor, factorp)
         return carry
 
-    lax.fori_loop(0, 3, near, 0)
+    lax.fori_loop(0, 3, near, 0, unroll=True)
     b_one(0)
     b_one(1)
 
@@ -564,7 +574,7 @@
         block(lax.rem(yy + y + 3, 4), 1 - l, factor, factorp)
         return carry
 
-    lax.fori_loop(0, 3, rest, 0)
+    lax.fori_loop(0, 3, rest, 0, unroll=True)
     a_direct(0)
     b_direct(0)
     z_step(OWN, 3)
@@ -575,6 +585,8 @@
     z_step(OTHER, 4)
     a_two(1)
     b_two(1)
+    drain(before)
+    first = len(sent)
     a_three(0)
     b_three(0)
     z_step(OWN, 4)
@@ -583,12 +595,13 @@
     a_three(1)
     b_three(1)
     gi_ref[h] = z_final(OWN)
+    drain(first)
     a_four(0)
     b_four(0)
+    a_four(1)
+    b_four(1)
     ex_wait(4)
     gi_ref[oh] = gir[...]
-    a_four(1)
-    b_four(1)
     for copy in sent:
         copy.wait_send()
 

time: 97.9 us -> 96.8 us (0.989)
  Pallas kernels: 97.1 us -> 96 us
    pallas_call x1, Pallas kernels: 95.1 us -> 94 us  [per_device(): pl.pallas_call(kernel, out_shape=(jax.ShapeDtypeStruct((288, 256), F32),...]
where the time goes in v5:
time: 96.8 us; the launch traced here: 96.6 us
  Pallas kernels  96 us (99%)
    pallas_call x1, Pallas kernels, per_device(): pl.pallas_call(kernel, out_shape=(jax.ShapeDtypeStruct((288, 256), F32),...  94 us
    pallas_call x1, Pallas kernels, per_device(): pl.pallas_call(finish, out_shape=(jax.ShapeDtypeStruct((288, 256), F32),...  2 us

profile of v5, /device:TPU:1, one launch (start us, length us, event | category | flops | bytes accessed | tf_op | source)
XLA Modules:
  0.0 96.6 jit_solution(2148560733359776562)
XLA Ops:
  0.6 94.0 %clipped_grads.1 = (f32[288,256]{1,0:T(8,128)}, f32[288,128]{1,0:T(8,128)}, bf16[2,16,4608]{2,1,0:T(8,128)(2,1)}) custom-call(f32[2]{0:T(128)} %lw_ref.1, s32[2]{0:T(128)} %len_ref.1, bf16[2,16,4608]{2,1,0:T(8,128)(2,1)} %x_ref.1, bf16[2,16,4608]{2,1,0:T(8,128)(2,1)} %g_ref.1, bf16[2,256,256]{2,1,0:T(8,128)(2,1)} %q_ref.1, bf16[2,256,128]{2,1,0:T(8,128)(2,1)} %k_ref.1, ...), custom_call_target="tpu_custom_call" | custom-call | flops 5000000000 | bytes 12000000 | tf_op jit(solution)/shard_map/clipped_grads/pallas_call | solution.py:624
  94.6 2.0 %finish.1 = (f32[288,256]{1,0:T(8,128)}, f32[288,128]{1,0:T(8,128)}, bf16[2,16,4608]{2,1,0:T(8,128)(2,1)}) custom-call(f32[288,256]{1,0:T(8,128)} %get-tuple-element.9.outt_ref, f32[288,128]{1,0:T(8,128)} %get-tuple-element.10.val_ref, bf16[2,16,4608]{2,1,0:T(8,128)(2,1)} %get-tuple-element.11.gi_ref), custom_call_target="tpu_custom_call" | custom-call | tf_op jit(solution)/shard_map/finish/pallas_call | solution.py:651

commit v6 on v5

--- a/solution.py
+++ b/solution.py
@@ -476,11 +476,11 @@
     local[2].wait()
     softmax(h)
     pl.semaphore_wait(barrier, len(peers))
+    ag_send(G, OWN, 1)
     ex_send(1, gsend)
-    ag_send(G, OWN, 1)
-    w_first(1)
     local[0].wait()
     ag_send(X, OWN, 1)
+    w_first(1)
     ag_next(G, OWN, 1)
     ex_send(0, x_ref.at[oh])
     ex_wait(1)

time: 96.8 us -> 96.8 us (level)
  no operation moved by 1% of the time
where the time goes in v6:
time: 96.8 us; the launch traced here: 96.6 us
  Pallas kernels  96 us (99%)
    pallas_call x1, Pallas kernels, per_device(): pl.pallas_call(kernel, out_shape=(jax.ShapeDtypeStruct((288, 256), F32),...  94 us
    pallas_call x1, Pallas kernels, per_device(): pl.pallas_call(finish, out_shape=(jax.ShapeDtypeStruct((288, 256), F32),...  2 us

profile of v6, /device:TPU:1, one launch (start us, length us, event | category | flops | bytes accessed | tf_op | source)
XLA Modules:
  0.0 96.6 jit_solution(14897758409973694867)
XLA Ops:
  0.6 94.0 %clipped_grads.1 = (f32[288,256]{1,0:T(8,128)}, f32[288,128]{1,0:T(8,128)}, bf16[2,16,4608]{2,1,0:T(8,128)(2,1)}) custom-call(f32[2]{0:T(128)} %lw_ref.1, s32[2]{0:T(128)} %len_ref.1, bf16[2,16,4608]{2,1,0:T(8,128)(2,1)} %x_ref.1, bf16[2,16,4608]{2,1,0:T(8,128)(2,1)} %g_ref.1, bf16[2,256,256]{2,1,0:T(8,128)(2,1)} %q_ref.1, bf16[2,256,128]{2,1,0:T(8,128)(2,1)} %k_ref.1, ...), custom_call_target="tpu_custom_call" | custom-call | flops 5000000000 | bytes 12000000 | tf_op jit(solution)/shard_map/clipped_grads/pallas_call | solution.py:624
  94.6 2.0 %finish.1 = (f32[288,256]{1,0:T(8,128)}, f32[288,128]{1,0:T(8,128)}, bf16[2,16,4608]{2,1,0:T(8,128)(2,1)}) custom-call(f32[288,256]{1,0:T(8,128)} %get-tuple-element.9.outt_ref, f32[288,128]{1,0:T(8,128)} %get-tuple-element.10.val_ref, bf16[2,16,4608]{2,1,0:T(8,128)(2,1)} %get-tuple-element.11.gi_ref), custom_call_target="tpu_custom_call" | custom-call | tf_op jit(solution)/shard_map/finish/pallas_call | solution.py:651
